TPU v7x, 32 devices: a whole 2x2x4 slice. The times are simulated.
32 devices in a mesh: section: 2 (over x), seq: 4 (over y, core), fsdp: 4 (over z).
Axes of the slice: x: 2, y: 2, z: 4, core: 2. Of those that a mesh axis runs over, the one named last changes fastest.
Arguments:
- boundary: bfloat16 [2, 24, 256, 768], P('section', 'fsdp', 'seq'), may hold values from -6 to 6
- timestep: int32 [24], P('fsdp'), may hold values from 0 to 999
- label: int32 [24], P('fsdp'), may hold values from 0 to 999
- label_table: bfloat16 [1000, 768], replicated, may hold values from -6 to 6
- ada_weight: bfloat16 [2, 768, 4608], P('section', 'fsdp'), may hold values from -0.21875 to 0.21875
- qkv_weight: bfloat16 [2, 768, 2304], P('section', 'fsdp'), may hold values from -0.21875 to 0.21875
- out_weight: bfloat16 [2, 768, 768], P('section', 'fsdp'), may hold values from -1.75 to 1.75
- up_weight: bfloat16 [2, 768, 3072], P('section', 'fsdp'), may hold values from -0.21875 to 0.21875
- down_weight: bfloat16 [2, 3072, 768], P('section', 'fsdp'), may hold values from -0.109375 to 0.109375
Outputs:
- end_rows: float32 [2, 24, 256, 768], P('section', 'fsdp', 'seq')
- cond_grad: float32 [2, 24, 768], P('section', 'fsdp')
- grad_ada: float32 [2, 768, 4608], P('section', 'fsdp', 'seq')
- grad_qkv: float32 [2, 768, 2304], P('section', 'fsdp')
- grad_out: float32 [2, 768, 768], P('section', 'fsdp')
- grad_up: float32 [2, 768, 3072], P('section', 'fsdp')
- grad_down: float32 [2, 3072, 768], P('section', 'fsdp')
All inputs are finite; a program needn't handle non-finite values.
Results may differ from a plain program's by a relative error of at most 0.023.
Values may be sent and summed in bfloat16 or wider, within the bound.
No kernel may reach another device: no remote copies, remote signals or barrier semaphores. Data moves between devices by JAX's collectives and lax.ppermute only.
A program may use at most 256 MiB of HBM per device.

v0:
```python
import math

import jax
import jax.numpy as jnp
from jax import lax
from jax.sharding import PartitionSpec as P

D = 768
HD = 64
MB = 6


EPS = 1e-06


def from_behind(block, axis, distance):
    devices = range(lax.axis_size(axis))
    route = [(i - distance, i) for i in devices if i - distance in devices]
    return lax.ppermute(block, axis, route)


def embed_time(timestep, model_width):
    half_width = model_width // 2
    frequency = jnp.exp(-math.log(10000.0) * jnp.arange(half_width, dtype=jnp.float32) / half_width)
    angles = timestep.astype(jnp.float32)[:, None] * frequency[None, :]
    return jnp.concatenate([jnp.cos(angles), jnp.sin(angles)], axis=1)


def normalize(array_in):
    centered = array_in - jnp.mean(array_in, axis=-1, keepdims=True)
    inv_std = lax.rsqrt(jnp.mean(centered * centered, axis=-1, keepdims=True) + EPS)
    return (centered * inv_std, inv_std)


def normalize_back(grad_in, normed, inv_std):
    return inv_std * (
        grad_in
        - jnp.mean(grad_in, axis=-1, keepdims=True)
        - normed * jnp.mean(grad_in * normed, axis=-1, keepdims=True)
    )


def gelu_tanh(array_in):
    return jax.nn.gelu(array_in, approximate=True)


def split_modulation(modulation, model_width):
    return [
        modulation[:, None, part_no * model_width : (part_no + 1) * model_width]
        for part_no in range(6)
    ]


def forward_layer(input_rows, modulation, weight_collection, groups):
    query_key_value_weight, output_weight, up_matrix, down_matrix = weight_collection
    latents_here, local_tokens, model_width = input_rows.shape
    shift_one, scale_one, gate_one, shift_two, scale_two, gate_two = split_modulation(
        modulation, model_width
    )
    score_scale = 1.0 / math.sqrt(HD)
    normed_one, rstd_one = normalize(input_rows)
    attn_in = (normed_one * (1.0 + scale_one) + shift_one).astype(jnp.bfloat16)
    qkv_rows = jnp.einsum(
        "lsd,de->lse", attn_in, query_key_value_weight, preferred_element_type=jnp.float32
    ).astype(jnp.bfloat16)
    split_qkv = qkv_rows.reshape(latents_here, local_tokens, 3, groups, model_width // groups)
    head_rows = lax.all_to_all(split_qkv, "seq", split_axis=3, concat_axis=1, tiled=True)
    full_tokens = head_rows.shape[1]
    heads_here = model_width // groups // HD
    queries = head_rows[:, :, 0, 0].reshape(latents_here, full_tokens, heads_here, HD)
    key_heads = head_rows[:, :, 1, 0].reshape(latents_here, full_tokens, heads_here, HD)
    value_heads = head_rows[:, :, 2, 0].reshape(latents_here, full_tokens, heads_here, HD)
    scores = (
        jnp.einsum("lqhe,lkhe->lhqk", queries, key_heads, preferred_element_type=jnp.float32)
        * score_scale
    )
    row_max = jnp.max(scores, axis=-1, keepdims=True)
    row_total = jnp.sum(jnp.exp(scores - row_max), axis=-1, keepdims=True)
    log_total = row_max + jnp.log(row_total)
    soft_weights = jnp.exp(scores - log_total).astype(jnp.bfloat16)
    head_out = jnp.einsum(
        "lhqk,lkhe->lqhe", soft_weights, value_heads, preferred_element_type=jnp.float32
    ).astype(jnp.bfloat16)
    head_out = head_out.reshape(latents_here, full_tokens, 1, model_width // groups)
    attended = lax.all_to_all(head_out, "seq", split_axis=1, concat_axis=2, tiled=True).reshape(
        latents_here, local_tokens, model_width
    )
    projected = jnp.einsum(
        "lsd,de->lse", attended, output_weight, preferred_element_type=jnp.float32
    )
    midway = input_rows + gate_one * projected
    normed_two, rstd_two = normalize(midway)
    perceptron_input = (normed_two * (1.0 + scale_two) + shift_two).astype(jnp.bfloat16)
    hidden_before = jnp.einsum(
        "zwt,tj->zwj", perceptron_input, up_matrix, preferred_element_type=jnp.float32
    )
    hidden_state = gelu_tanh(hidden_before).astype(jnp.bfloat16)
    perceptron_output = jnp.einsum(
        "eyq,qb->eyb", hidden_state, down_matrix, preferred_element_type=jnp.float32
    )
    result = midway + gate_two * perceptron_output
    saved_state = (
        normed_one,
        rstd_one,
        attn_in,
        queries,
        key_heads,
        value_heads,
        log_total,
        attended,
        projected,
        normed_two,
        rstd_two,
        perceptron_input,
        hidden_before,
        hidden_state,
        perceptron_output,
    )
    return (result, saved_state)


def backward_layer(grad_out, saved_state, modulation, weight_collection, groups):
    query_key_value_weight, output_weight, up_matrix, down_matrix = weight_collection
    (
        normed_one,
        rstd_one,
        attn_in,
        queries,
        key_heads,
        value_heads,
        log_total,
        attended,
        projected,
        normed_two,
        rstd_two,
        perceptron_input,
        hidden_before,
        hidden_state,
        perceptron_output,
    ) = saved_state
    latents_here, local_tokens, model_width = grad_out.shape
    shift_one, scale_one, gate_one, shift_two, scale_two, gate_two = split_modulation(
        modulation, model_width
    )
    score_scale = 1.0 / math.sqrt(HD)
    perceptron_gradient = (gate_two * grad_out).astype(jnp.bfloat16)
    d_gate_two = jnp.sum(grad_out * perceptron_output, axis=1)
    down_gradient = jnp.einsum(
        "ubx,ubp->xp", hidden_state, perceptron_gradient, preferred_element_type=jnp.float32
    )
    hidden_gradient = jnp.einsum(
        "zeo,bo->zeb", perceptron_gradient, down_matrix, preferred_element_type=jnp.float32
    )
    prior_gradient = jax.vjp(gelu_tanh, hidden_before)[1](hidden_gradient)[0].astype(jnp.bfloat16)
    up_gradient = jnp.einsum(
        "izp,izn->pn", perceptron_input, prior_gradient, preferred_element_type=jnp.float32
    )
    perceptron_input_gradient = jnp.einsum(
        "mwz,bz->mwb", prior_gradient, up_matrix, preferred_element_type=jnp.float32
    )
    d_shift_two = jnp.sum(perceptron_input_gradient, axis=1)
    d_scale_two = jnp.sum(perceptron_input_gradient * normed_two, axis=1)
    d_midway = grad_out + normalize_back(
        perceptron_input_gradient * (1.0 + scale_two), normed_two, rstd_two
    )
    d_proj = (gate_one * d_midway).astype(jnp.bfloat16)
    d_gate_one = jnp.sum(d_midway * projected, axis=1)
    g_out = jnp.einsum("lsd,lse->de", attended, d_proj, preferred_element_type=jnp.float32)
    d_attended = jnp.einsum(
        "lse,de->lsd", d_proj, output_weight, preferred_element_type=jnp.float32
    ).astype(jnp.bfloat16)
    d_split = d_attended.reshape(latents_here, local_tokens, groups, model_width // groups)
    d_heads = lax.all_to_all(d_split, "seq", split_axis=2, concat_axis=1, tiled=True)
    full_tokens = d_heads.shape[1]
    heads_here = model_width // groups // HD
    d_heads = d_heads.reshape(latents_here, full_tokens, heads_here, HD)
    scores = (
        jnp.einsum("lqhe,lkhe->lhqk", queries, key_heads, preferred_element_type=jnp.float32)
        * score_scale
    )
    soft_full = jnp.exp(scores - log_total)
    d_probs = jnp.einsum(
        "lqhe,lkhe->lhqk", d_heads, value_heads, preferred_element_type=jnp.float32
    )
    row_delta = jnp.sum(soft_full * d_probs, axis=-1, keepdims=True)
    d_scores = (soft_full * (d_probs - row_delta)).astype(jnp.bfloat16)
    d_queries = (
        jnp.einsum("lhqk,lkhe->lqhe", d_scores, key_heads, preferred_element_type=jnp.float32)
        * score_scale
    ).astype(jnp.bfloat16)
    d_keys = (
        jnp.einsum("lhqk,lqhe->lkhe", d_scores, queries, preferred_element_type=jnp.float32)
        * score_scale
    ).astype(jnp.bfloat16)
    d_values = jnp.einsum(
        "lhqk,lqhe->lkhe",
        soft_full.astype(jnp.bfloat16),
        d_heads,
        preferred_element_type=jnp.float32,
    ).astype(jnp.bfloat16)
    stacked = jnp.stack([d_queries, d_keys, d_values], axis=2).reshape(
        latents_here, full_tokens, 3, 1, model_width // groups
    )
    d_qkv = lax.all_to_all(stacked, "seq", split_axis=1, concat_axis=3, tiled=True).reshape(
        latents_here, local_tokens, 3 * model_width
    )
    g_qkv = jnp.einsum("lsd,lse->de", attn_in, d_qkv, preferred_element_type=jnp.float32)
    d_attn_in = jnp.einsum(
        "lse,de->lsd", d_qkv, query_key_value_weight, preferred_element_type=jnp.float32
    )
    d_shift_one = jnp.sum(d_attn_in, axis=1)
    d_scale_one = jnp.sum(d_attn_in * normed_one, axis=1)
    d_inputs = d_midway + normalize_back(d_attn_in * (1.0 + scale_one), normed_one, rstd_one)
    d_part = jnp.concatenate(
        [d_shift_one, d_scale_one, d_gate_one, d_shift_two, d_scale_two, d_gate_two], axis=1
    )
    return (d_inputs, d_part, (g_qkv, g_out, up_gradient, down_gradient))


def body(
    boundary,
    timestep,
    label,
    label_table,
    ada_weight,
    qkv_weight,
    out_weight,
    up_weight,
    down_weight,
):
    section_index = lax.axis_index("section")
    on_first = section_index == 0
    groups = lax.axis_size("seq")
    seq_index = lax.axis_index("seq")
    adaptive_weight, query_key_value_weight, output_weight, up_matrix, down_matrix = (
        lax.all_gather(ada_weight[0], "fsdp", axis=0, tiled=True),
        lax.all_gather(qkv_weight[0], "fsdp", axis=0, tiled=True),
        lax.all_gather(out_weight[0], "fsdp", axis=0, tiled=True),
        lax.all_gather(up_weight[0], "fsdp", axis=0, tiled=True),
        lax.all_gather(down_weight[0], "fsdp", axis=0, tiled=True),
    )
    weight_collection = (query_key_value_weight, output_weight, up_matrix, down_matrix)
    ada_cols = adaptive_weight.shape[1] // groups
    condition_vector = embed_time(timestep, D) + jnp.take(label_table, label, axis=0).astype(
        jnp.float32
    )
    silu_cond = jax.nn.silu(condition_vector).astype(jnp.bfloat16)
    modulation = jnp.dot(silu_cond, adaptive_weight, preferred_element_type=jnp.float32)
    own_rows = boundary[0].astype(jnp.float32)
    per_micro = own_rows.shape[0] // MB
    received = jnp.zeros_like(own_rows[:per_micro])
    saved_list = []
    outputs = []
    for fwd_step in range(MB + 1):
        mb_index = jnp.clip(fwd_step - section_index, 0, MB - 1)
        mod_rows = lax.dynamic_slice_in_dim(modulation, mb_index * per_micro, per_micro, 0)
        static_row = min(fwd_step, MB - 1) * per_micro
        layer_in = jnp.where(on_first, own_rows[static_row : static_row + per_micro], received)
        result, saved_state = forward_layer(layer_in, mod_rows, weight_collection, groups)
        saved_list.append(saved_state)
        outputs.append(result)
        if fwd_step < MB:
            received = from_behind(result.astype(jnp.bfloat16), "section", 1).astype(jnp.float32)
    ada_total = jnp.zeros((adaptive_weight.shape[0], ada_cols), jnp.float32)
    totals = [jnp.zeros(weight_matrix.shape, jnp.float32) for weight_matrix in weight_collection]
    incoming = jnp.zeros_like(own_rows[:per_micro])
    grads_in = []
    cond_back = []
    for back_step in range(MB + 1):
        saved_state = saved_list[MB - back_step]
        mb_index = jnp.clip(MB - back_step - section_index, 0, MB - 1)
        mod_rows = lax.dynamic_slice_in_dim(modulation, mb_index * per_micro, per_micro, 0)
        loss_micro = MB - 1 - back_step
        if loss_micro >= 0:
            from_loss = own_rows[loss_micro * per_micro : (loss_micro + 1) * per_micro]
        else:
            from_loss = jnp.zeros_like(incoming)
        grad_out = jnp.where(on_first, incoming, from_loss)
        d_inputs, d_part, layer_grads = backward_layer(
            grad_out, saved_state, mod_rows, weight_collection, groups
        )
        d_mod = lax.psum(d_part, "seq").astype(jnp.bfloat16)
        silu_rows = lax.dynamic_slice_in_dim(silu_cond, mb_index * per_micro, per_micro, 0)
        cond_rows = lax.dynamic_slice_in_dim(condition_vector, mb_index * per_micro, per_micro, 0)
        mod_cols = lax.dynamic_slice_in_dim(d_mod, seq_index * ada_cols, ada_cols, 1)
        ada_total = ada_total + jnp.einsum(
            "ld,le->de", silu_rows, mod_cols, preferred_element_type=jnp.float32
        )
        for grad_no in range(4):
            totals[grad_no] = totals[grad_no] + layer_grads[grad_no]
        d_silu = jnp.einsum("le,de->ld", d_mod, adaptive_weight, preferred_element_type=jnp.float32)
        d_cond = jax.vjp(jax.nn.silu, cond_rows)[1](d_silu)[0]
        grads_in.append(d_inputs)
        cond_back.append(d_cond)
        if back_step < MB:
            incoming = from_behind(d_inputs.astype(jnp.bfloat16), "section", -1).astype(jnp.float32)
    end_rows = jnp.concatenate(
        [jnp.where(on_first, grads_in[MB - micro], outputs[micro + 1]) for micro in range(MB)],
        axis=0,
    )[None]
    cond_grad = jnp.concatenate(
        [
            jnp.where(on_first, cond_back[MB - micro], cond_back[MB - 1 - micro])
            for micro in range(MB)
        ],
        axis=0,
    )[None]
    shares = (
        lax.psum_scatter(ada_total, "fsdp", scatter_dimension=0, tiled=True),
        lax.psum_scatter(totals[0], "fsdp", scatter_dimension=0, tiled=True),
        lax.psum_scatter(totals[1], "fsdp", scatter_dimension=0, tiled=True),
        lax.psum_scatter(totals[2], "fsdp", scatter_dimension=0, tiled=True),
        lax.psum_scatter(totals[3], "fsdp", scatter_dimension=0, tiled=True),
    )
    ada_share = shares[0]
    reduced = lax.psum((shares[1], shares[2], shares[3], shares[4]), "seq")
    return (
        end_rows,
        cond_grad,
        ada_share[None],
        reduced[0][None],
        reduced[1][None],
        reduced[2][None],
        reduced[3][None],
    )


def solution(mesh):
    placed = (
        P("section", "fsdp", "seq", None),
        P("fsdp"),
        P("fsdp"),
        P(),
        P("section", "fsdp", None),
        P("section", "fsdp", None),
        P("section", "fsdp", None),
        P("section", "fsdp", None),
        P("section", "fsdp", None),
    )
    return jax.shard_map(
        body,
        mesh=mesh,
        in_specs=placed,
        out_specs=(
            P("section", "fsdp", "seq", None),
            P("section", "fsdp", None),
            P("section", "fsdp", "seq"),
            P("section", "fsdp", None),
            P("section", "fsdp", None),
            P("section", "fsdp", None),
            P("section", "fsdp", None),
        ),
        check_vma=False,
    )
```

profile of v0, /device:TPU:0, one launch (start us, length us, event | category | flops | bytes accessed | tf_op | source)
XLA Modules:
  0.0 1802.0 jit_solution(1822898205449675086)
XLA Ops:
  13.6 127.0 %all-gather.11.cloned.1.call-done = bf16[1,768,4608]{2,1,0:T(8,128)(2,1)} async-done(((bf16[1,192,4608]{2,1,0:T(8,128)(2,1)}), bf16[1,768,4608]{2,1,0:T(8,128)(2,1)}) %all-gather.11.cloned.1.call-update) | async-done | bytes 7077904 | tf_op jit(solution)/shard_map/all_gather | solution.py:236
  145.7 64.7 %all-gather.13.cloned.1.call-done = bf16[1,768,2304]{2,1,0:T(8,128)(2,1)} async-done(((bf16[1,192,2304]{2,1,0:T(8,128)(2,1)}), bf16[1,768,2304]{2,1,0:T(8,128)(2,1)}) %all-gather.13.cloned.1.call-update) | async-done | bytes 3538960 | tf_op jit(solution)/shard_map/all_gather | solution.py:237
  213.6 10.0 all_to_all.441
  227.2 6.7 all_to_all.442
  234.3 6.7 all-gather.15.cloned.1.call-done
  243.6 87.4 %all-gather.17.cloned.1.call-done = bf16[1,768,3072]{2,1,0:T(8,128)(2,1)} async-done(((bf16[1,192,3072]{2,1,0:T(8,128)(2,1)}), bf16[1,768,3072]{2,1,0:T(8,128)(2,1)}) %all-gather.17.cloned.1.call-update) | async-done | bytes 4718608 | tf_op jit(solution)/shard_map/all_gather | solution.py:239
  335.2 85.1 %all-gather.19.cloned.1.call-done = bf16[1,3072,768]{2,1,0:T(8,128)(2,1)} async-done(((bf16[1,768,768]{2,1,0:T(8,128)(2,1)}), bf16[1,3072,768]{2,1,0:T(8,128)(2,1)}) %all-gather.19.cloned.1.call-update) | async-done | bytes 4718608 | tf_op jit(solution)/shard_map/all_gather | solution.py:240
  420.3 4.4 fusion.329
  432.0 10.0 all_to_all.443
  447.2 6.9 all_to_all.444
  462.5 4.3 collective-permute-start.1
  471.1 9.8 all_to_all.445
  487.7 7.3 all_to_all.446
  514.5 9.8 all_to_all.447
  536.4 8.7 all_to_all.448
  567.8 9.8 all_to_all.449
  589.7 8.3 all_to_all.450
  620.9 9.8 all_to_all.451
  642.8 8.4 all_to_all.452
  673.3 9.8 all_to_all.453
  691.5 7.3 all_to_all.454
  716.5 7.9 all_to_all.455
  736.7 11.2 all_to_all.456
  758.4 5.2 collective-permute-done.6
  772.8 7.7 all_to_all.457
  792.8 11.4 all_to_all.458
  815.6 4.8 collective-permute-done.7
  829.5 7.7 all_to_all.459
  849.5 11.4 all_to_all.460
  871.9 5.2 collective-permute-done.8
  886.3 7.8 all_to_all.461
  913.3 7.0 all-to-all-done.21
  932.6 5.3 fusion.521
  970.9 4.4 all-to-all-start.23
  975.4 5.1 fusion.527
  1043.8 6.0 all-to-all-done.25
  1078.0 5.1 fusion.533
  1092.0 5.1 fusion.545
  1110.4 4.7 all-to-all-done.27
  1115.8 17.7 add_add_fusion.2
  1137.5 5.1 fusion.562
  1142.6 5.1 fusion.561
  1147.7 5.1 fusion.560
  1152.9 5.1 fusion.559
  1158.0 5.0 fusion.558
  1163.0 20.6 %add_add_fusion = f32[3072,768]{1,0:T(8,128)} fusion(f32[3072,768]{1,0:T(8,128)} %fusion.558, f32[3072,768]{1,0:T(8,128)} %fusion.559, f32[3072,768]{1,0:T(8,128)} %fusion.560, f32[3072,768]{1,0:T(8,128)} %fusion.561, f32[3072,768]{1,0:T(8,128)S(1)} %fusion.409, f32[3072,768]{1,0:T(8,128)} %fusion.562, bf16[1,64,768]{2,1,0:T(8,128)(2,1)S(1)} %copy-done.175, ...), kind=kOutput, calls=%fused_computation.1 | convolution fusion | flops 318111744 | bytes 66948096 | tf_op jit(solution)/shard_map/ubx,ubp->xp/dot_general | solution.py:148
  1187.1 5.1 fusion.524
  1192.3 5.1 fusion.530
  1197.5 5.2 fusion.536
  1202.7 5.1 fusion.542
  1207.9 5.1 fusion.548
  1213.0 20.5 %add_add_fusion.1 = f32[768,3072]{1,0:T(8,128)} fusion(f32[768,3072]{1,0:T(8,128)} %fusion.548, f32[768,3072]{1,0:T(8,128)} %fusion.542, f32[768,3072]{1,0:T(8,128)} %fusion.536, f32[768,3072]{1,0:T(8,128)} %fusion.530, f32[768,3072]{1,0:T(8,128)S(1)} %fusion.518, f32[768,3072]{1,0:T(8,128)} %fusion.524, bf16[64,3072]{1,0:T(8,128)(2,1)} %copy-done.93, ...), kind=kOutput, calls=%fused_computation.2 | convolution fusion | flops 316391424 | bytes 66656768 | tf_op jit(solution)/shard_map/izp,izn->pn/dot_general | solution.py:155
  1235.6 4.6 fusion.254
  1243.8 23.0 %all-reduce = (bf16[1,4608]{1,0:T(2,128)(2,1)S(1)}, bf16[1,4608]{1,0:T(2,128)(2,1)S(1)}, bf16[1,4608]{1,0:T(2,128)(2,1)S(1)}, bf16[1,4608]{1,0:T(2,128)(2,1)S(1)...) all-reduce(f32[1,4608]{1,0:T(1,128)S(1)} %constant_dynamic-update-s, ...), channel_id=1, replica_groups=mesh['section'=2,'seq'=4,'fsdp'=4] {'seq'}, use_global_device_ids=true, to_apply=%region_90.91 | all-reduce | flops 32256 | bytes 193536 | tf_op jit(solution)/shard_map/psum | solution.py:282
  1270.5 5.0 fusion.429
  1275.5 4.9 fusion.431
  1280.5 4.9 fusion.433
  1285.4 132.7 %reduce-scatter.14.cloned.1.call-done = f32[768,768]{1,0:T(8,128)} async-done(((f32[3072,768]{1,0:T(8,128)}), f32[768,768]{1,0:T(8,128)}) %reduce-scatter.14.cloned.1.call-update) | async-done | bytes 2359312 | tf_op jit(solution)/shard_map/reduce_scatter | solution.py:313
  1418.1 164.5 %reduce-scatter.12.cloned.1.call-done = f32[192,3072]{1,0:T(8,128)} async-done(((f32[768,3072]{1,0:T(8,128)}), f32[192,3072]{1,0:T(8,128)}) %reduce-scatter.12.cloned.1.call-update) | async-done | bytes 2359312 | tf_op jit(solution)/shard_map/reduce_scatter | solution.py:312
  1582.7 5.1 fusion.2
  1587.7 5.1 broadcast_select_fusion.5
  1592.8 5.0 broadcast_select_fusion
  1611.0 41.6 %reduce-scatter.6.cloned.1.call-done = f32[192,1152]{1,0:T(8,128)} async-done(((f32[768,1152]{1,0:T(8,128)}), f32[192,1152]{1,0:T(8,128)}) %reduce-scatter.6.cloned.1.call-update) | async-done | bytes 884752 | tf_op jit(solution)/shard_map/reduce_scatter | solution.py:309
  1652.6 135.8 %all-reduce.4.cloned.1.call-done = (f32[1,192,2304]{2,1,0:T(8,128)}, f32[1,192,768]{2,1,0:T(8,128)}, f32[1,192,3072]{2,1,0:T(8,128)}, f32[1,768,768]{2,1,0:T(8,128)}) async-done(((f32[1,192,2304]{2,1,0:T(8,128)}, f32[1,192,768]{2,1,0:T(8,128)}, f32[1,192,3072]{2,1,0:T(8,128)}, f32[1,768,768]{2,1,0:T(8,128)}), (f32[1,192,2304]{2,1,0:T(8,128)}, f32[1,192,768]{2,1,0:T(8,128)}, f32[1,192,3072]{2,1,0:T(8,128)}, ...) | async-done | bytes 7077904 | tf_op jit(solution)/shard_map/psum | solution.py:316
  (1357 shorter events, 514.3 us)
Async XLA Ops:
  7.2 133.3 %all-gather.11.cloned.1.call-start = ((), (), s32[]{:S(2)}) async-start(), calls=%async_computation.38 | async-start | bytes 8847360 | tf_op jit(solution)/shard_map/all_gather | solution.py:236
  7.9 202.4 %all-gather.13.cloned.1.call-start = ((), (), s32[]{:S(2)}) async-start(), calls=%async_computation.39 | async-start | bytes 4423680 | tf_op jit(solution)/shard_map/all_gather | solution.py:237
  8.7 232.3 %all-gather.15.cloned.1.call-start = ((), (), s32[]{:S(2)}) async-start(), calls=%async_computation.40 | async-start | bytes 1474560 | tf_op jit(solution)/shard_map/all_gather | solution.py:238
  9.4 321.6 %all-gather.17.cloned.1.call-start = ((), (), s32[]{:S(2)}) async-start(), calls=%async_computation.41 | async-start | bytes 5898240 | tf_op jit(solution)/shard_map/all_gather | solution.py:239
  10.0 410.3 %all-gather.19.cloned.1.call-start = ((), (), s32[]{:S(2)}) async-start(), calls=%async_computation.42 | async-start | bytes 5898240 | tf_op jit(solution)/shard_map/all_gather | solution.py:240
  11.8 1104.0 %copy-start.10 = (f32[1,6,64,768]{3,2,1,0:T(8,128)}, f32[1,6,64,768]{3,2,1,0:T(8,128)S(1)}, u32[]{:S(2)}) copy-start(f32[1,6,64,768]{3,2,1,0:T(8,128)S(1)} %convert_element_type.617) | copy-start | bytes 3538948
  12.6 197.8 %copy-start.356 = (f32[64]{0:T(128)}, f32[64]{0:T(128)S(1)}, u32[]{:S(2)}) copy-start(f32[64]{0:T(128)S(1)} %broadcast_multiply_fusion.41) | copy-start | bytes 772
  12.8 197.6 %copy-start.363 = (f32[64]{0:T(128)}, f32[64]{0:T(128)S(1)}, u32[]{:S(2)}) copy-start(f32[64]{0:T(128)S(1)} %add_rsqrt_fusion.13) | copy-start | bytes 772
  13.6 131.0 %copy-start.176 = (bf16[6,768]{1,0:T(8,128)(2,1)}, bf16[6,768]{1,0:T(8,128)(2,1)S(1)}, u32[]{:S(2)}) copy-start(bf16[6,768]{1,0:T(8,128)(2,1)S(1)} %get-tuple-element.200) | copy-start | bytes 27652
  145.6 78.0 %copy-start.199 = (f32[768]{0:T(1024)}, f32[768]{0:T(1024)S(1)}, u32[]{:S(2)}) copy-start(f32[768]{0:T(1024)S(1)} %get-tuple-element.123) | copy-start | bytes 9220
  145.7 78.0 %copy-start.243 = (f32[768]{0:T(1024)}, f32[768]{0:T(1024)S(1)}, u32[]{:S(2)}) copy-start(f32[768]{0:T(1024)S(1)} %get-tuple-element.122) | copy-start | bytes 9220
  145.7 95.4 %copy-start.223 = (f32[768]{0:T(1024)}, f32[768]{0:T(1024)S(1)}, u32[]{:S(2)}) copy-start(f32[768]{0:T(1024)S(1)} %get-tuple-element.124) | copy-start | bytes 9220
  145.7 185.3 %copy-start.197 = (f32[768]{0:T(1024)}, f32[768]{0:T(1024)S(1)}, u32[]{:S(2)}) copy-start(f32[768]{0:T(1024)S(1)} %get-tuple-element.120) | copy-start | bytes 9220
  145.7 185.3 %copy-start.239 = (f32[768]{0:T(1024)}, f32[768]{0:T(1024)S(1)}, u32[]{:S(2)}) copy-start(f32[768]{0:T(1024)S(1)} %get-tuple-element.131) | copy-start | bytes 9220
  145.7 274.7 %copy-start.241 = (f32[768]{0:T(1024)}, f32[768]{0:T(1024)S(1)}, u32[]{:S(2)}) copy-start(f32[768]{0:T(1024)S(1)} %get-tuple-element.121) | copy-start | bytes 9220
  145.7 285.0 %copy-start.190 = (f32[768]{0:T(1024)}, f32[768]{0:T(1024)S(1)}, u32[]{:S(2)}) copy-start(f32[768]{0:T(1024)S(1)} %get-tuple-element.117) | copy-start | bytes 9220
  145.7 311.1 %copy-start.178 = (f32[768]{0:T(1024)}, f32[768]{0:T(1024)S(1)}, u32[]{:S(2)}) copy-start(f32[768]{0:T(1024)S(1)} %get-tuple-element.130) | copy-start | bytes 9220
  224.4 110.9 %copy-start.12 = (f32[3,256,256]{1,2,0:T(8,128)}, f32[3,256,256]{1,2,0:T(8,128)S(1)}, u32[]{:S(2)}) copy-start(f32[3,256,256]{1,2,0:T(8,128)S(1)} %get-tuple-element.231) | copy-start | bytes 2359300
  224.5 110.7 %copy-start.201 = (f32[3,256]{1,0:T(4,128)}, f32[3,256]{1,0:T(4,128)S(1)}, u32[]{:S(2)}) copy-start(f32[3,256]{1,0:T(4,128)S(1)} %log_add_fusion.6) | copy-start | bytes 9220
  234.3 100.9 %copy-start.105 = (bf16[64,768]{1,0:T(8,128)(2,1)}, bf16[64,768]{1,0:T(8,128)(2,1)S(1)}, u32[]{:S(2)}) copy-start(bf16[64,768]{1,0:T(8,128)(2,1)S(1)} %reshape.2236) | copy-start | bytes 294916
  243.4 181.3 %copy-start.62 = (f32[1,64,768]{2,1,0:T(8,128)}, f32[1,64,768]{2,1,0:T(8,128)S(1)}, u32[]{:S(2)}) copy-start(f32[1,64,768]{2,1,0:T(8,128)S(1)} %get-tuple-element.199) | copy-start | bytes 589828
  243.4 181.3 %copy-start.360 = (f32[64]{0:T(128)}, f32[64]{0:T(128)S(1)}, u32[]{:S(2)}) copy-start(f32[64]{0:T(128)S(1)} %broadcast_multiply_fusion.40) | copy-start | bytes 772
  243.6 181.1 %copy-start.367 = (f32[64]{0:T(128)}, f32[64]{0:T(128)S(1)}, u32[]{:S(2)}) copy-start(f32[64]{0:T(128)S(1)} %add_rsqrt_fusion.12) | copy-start | bytes 772
  424.7 5.6 collective-permute-start
  462.5 6.5 collective-permute-start.1
  504.3 6.5 collective-permute-start.2
  526.0 26.4 %copy-start.182 = (f32[768]{0:T(1024)S(1)}, f32[768]{0:T(1024)}, u32[]{:S(2)}) copy-start(f32[768]{0:T(1024)} %get-tuple-element.128) | copy-start | bytes 9220
  526.0 29.8 %slice-start.20 = ((s8[4718592]{0:T(1024)(128)(4,1)}), s8[524288]{0:T(1024)(128)(4,1)S(1)}, s32[]{:S(2)}) async-start(s8[4718592]{0:T(1024)(128)(4,1)} %bitcast.1286), calls=%async_computation.64 | async-start | bytes 1048576
  557.5 6.5 collective-permute-start.3
  579.3 26.3 %copy-start.184 = (f32[768]{0:T(1024)S(1)}, f32[768]{0:T(1024)}, u32[]{:S(2)}) copy-start(f32[768]{0:T(1024)} %get-tuple-element.127) | copy-start | bytes 9220
  579.3 29.7 %slice-start.22 = ((s8[4718592]{0:T(1024)(128)(4,1)}), s8[524288]{0:T(1024)(128)(4,1)S(1)}, s32[]{:S(2)}) async-start(s8[4718592]{0:T(1024)(128)(4,1)} %bitcast.1288), calls=%async_computation.66 | async-start | bytes 1048576
  610.7 6.5 collective-permute-start.4
  632.4 25.9 %copy-start.186 = (f32[768]{0:T(1024)S(1)}, f32[768]{0:T(1024)}, u32[]{:S(2)}) copy-start(f32[768]{0:T(1024)} %get-tuple-element.126) | copy-start | bytes 9220
  632.4 29.3 %slice-start.24 = ((s8[4718592]{0:T(1024)(128)(4,1)}), s8[524288]{0:T(1024)(128)(4,1)S(1)}, s32[]{:S(2)}) async-start(s8[4718592]{0:T(1024)(128)(4,1)} %bitcast.1290), calls=%async_computation.68 | async-start | bytes 1048576
  663.4 6.5 collective-permute-start.5
  670.0 30.1 %copy-start.41 = (f32[1,64,768]{2,1,0:T(8,128)}, f32[1,64,768]{2,1,0:T(8,128)S(1)}, u32[]{:S(2)}) copy-start(f32[1,64,768]{2,1,0:T(8,128)S(1)} %get-tuple-element.177) | copy-start | bytes 589828
  757.0 6.6 collective-permute-start.6
  792.7 31.8 %slice-start.4 = ((s8[4718592]{0:T(1024)(128)(4,1)}), s8[524288]{0:T(1024)(128)(4,1)S(1)}, s32[]{:S(2)}) async-start(s8[4718592]{0:T(1024)(128)(4,1)} %bitcast.1270), calls=%async_computation.48 | async-start | bytes 1048576
  813.9 6.5 collective-permute-start.7
  849.5 31.8 %slice-start.6 = ((s8[4718592]{0:T(1024)(128)(4,1)}), s8[524288]{0:T(1024)(128)(4,1)S(1)}, s32[]{:S(2)}) async-start(s8[4718592]{0:T(1024)(128)(4,1)} %bitcast.1272), calls=%async_computation.50 | async-start | bytes 1048576
  870.6 6.5 collective-permute-start.8
  907.2 13.1 all-to-all-start.21
  931.0 6.9 collective-permute-start.9
  946.8 8.6 all-to-all-start.22
  970.9 13.3 all-to-all-start.23
  994.9 6.6 collective-permute-start.10
  1013.4 8.6 all-to-all-start.24
  1036.7 13.1 all-to-all-start.25
  1040.9 244.6 %reduce-scatter.10.cloned.1.call-start = ((), (), s32[]{:S(2)}) async-start(), calls=%async_computation.35 | async-start | bytes 2949120 | tf_op jit(solution)/shard_map/reduce_scatter | solution.py:311
  1060.4 6.6 collective-permute-start.11
  1088.6 8.5 all-to-all-start.26
  1102.8 12.3 all-to-all-start.27
  1106.3 179.2 %reduce-scatter.8.cloned.1.call-start = ((), (), s32[]{:S(2)}) async-start(), calls=%async_computation.34 | async-start | bytes 8847360 | tf_op jit(solution)/shard_map/reduce_scatter | solution.py:310
  1133.6 284.5 %reduce-scatter.14.cloned.1.call-start = ((), (), s32[]{:S(2)}) async-start(), calls=%async_computation.37 | async-start | bytes 11796480 | tf_op jit(solution)/shard_map/reduce_scatter | solution.py:313
  1183.7 398.9 %reduce-scatter.12.cloned.1.call-start = ((), (), s32[]{:S(2)}) async-start(), calls=%async_computation.36 | async-start | bytes 11796480 | tf_op jit(solution)/shard_map/reduce_scatter | solution.py:312
  1233.8 418.8 %reduce-scatter.6.cloned.1.call-start = ((), (), s32[]{:S(2)}) async-start(), calls=%async_computation.33 | async-start | bytes 4423680 | tf_op jit(solution)/shard_map/reduce_scatter | solution.py:309
  1240.2 26.8 %copy-start.314 = (f32[768]{0:T(1024)S(1)}, f32[768]{0:T(1024)}, u32[]{:S(2)}) copy-start(f32[768]{0:T(1024)} %get-tuple-element.132) | copy-start | bytes 9220
  1240.2 26.8 %copy-start.315 = (f32[768]{0:T(1024)S(1)}, f32[768]{0:T(1024)}, u32[]{:S(2)}) copy-start(f32[768]{0:T(1024)} %get-tuple-element.133) | copy-start | bytes 9220
  1240.2 26.8 %copy-start.316 = (f32[768]{0:T(1024)S(1)}, f32[768]{0:T(1024)}, u32[]{:S(2)}) copy-start(f32[768]{0:T(1024)} %get-tuple-element.134) | copy-start | bytes 9220
  1240.3 26.8 %copy-start.317 = (f32[768]{0:T(1024)S(1)}, f32[768]{0:T(1024)}, u32[]{:S(2)}) copy-start(f32[768]{0:T(1024)} %get-tuple-element.135) | copy-start | bytes 9220
  1240.3 26.8 %copy-start.318 = (f32[768]{0:T(1024)S(1)}, f32[768]{0:T(1024)}, u32[]{:S(2)}) copy-start(f32[768]{0:T(1024)} %get-tuple-element.136) | copy-start | bytes 9220
  1240.3 26.8 %copy-start.319 = (f32[768]{0:T(1024)S(1)}, f32[768]{0:T(1024)}, u32[]{:S(2)}) copy-start(f32[768]{0:T(1024)} %get-tuple-element.137) | copy-start | bytes 9220
  1240.3 26.8 %copy-start.320 = (f32[768]{0:T(1024)S(1)}, f32[768]{0:T(1024)}, u32[]{:S(2)}) copy-start(f32[768]{0:T(1024)} %get-tuple-element.138) | copy-start | bytes 9220
  1270.5 518.0 %all-reduce.4.cloned.1.call-start = ((), (), s32[]{:S(2)}) async-start(), calls=%async_computation.43 | async-start | bytes 14155776 | tf_op jit(solution)/shard_map/psum | solution.py:316
  (367 other events, 2579.5 us)
Sparse Core Ops, SparseCore 0:
  9.6 130.8 all-gather.10
  142.1 68.2 all-gather.12
  211.9 29.0 all-gather.14
  242.4 88.5 all-gather.16
  332.4 87.8 all-gather.18
  1078.1 44.6 reduce-scatter.9
  1133.7 120.1 reduce-scatter.7
  1256.3 161.7 reduce-scatter.13
  1420.5 162.1 reduce-scatter.11
  1585.4 67.1 reduce-scatter.5
  1655.2 133.1 all-reduce.3
where the time goes:
time: 1820 us; the launch traced here: 1800 us
  waiting for transfers between devices  910 us (50%)
  matrix products  373 us (20%)
  blocking collectives  211 us (12%)
  local copies, waits for them, and re-layouts  136 us (7%)
  other arithmetic  89.9 us (5%)
  starting transfers between devices  62.2 us (3%)
  between operations  20.3 us (1%)
    reduce_scatter x1, waiting for transfers between devices, body(): lax.psum_scatter(totals[2], 'fsdp', scatter_dimension=0, tiled=True)  165 us
    psum x1, waiting for transfers between devices, body(): reduced = lax.psum((shares[1], shares[2], shares[3], shares[4]), 'seq')  136 us
    reduce_scatter x1, waiting for transfers between devices, body(): lax.psum_scatter(totals[3], 'fsdp', scatter_dimension=0, tiled=True)  133 us
    all_gather x1, waiting for transfers between devices, body(): lax.all_gather(ada_weight[0], 'fsdp', axis=0, tiled=True)  127 us
    all_gather x1, waiting for transfers between devices, body(): lax.all_gather(up_weight[0], 'fsdp', axis=0, tiled=True)  87.4 us
    all_gather x1, waiting for transfers between devices, body(): lax.all_gather(down_weight[0], 'fsdp', axis=0, tiled=True)  85.1 us
    all_to_all x7, blocking collectives, forward_layer(): lax.all_to_all(split_qkv, 'seq', split_axis=3, concat_axis=1, tiled=True)  69.2 us
    all_gather x1, waiting for transfers between devices, body(): lax.all_gather(qkv_weight[0], 'fsdp', axis=0, tiled=True)  64.7 us
  transfers between devices with their start and end apart: 30, of which 26 were waited for; matrix products, arithmetic and copies ran while one was open for 13% of the time, Pallas kernels for 0%

commit v1 on v0

v1 whole, which is shorter than its diff:
```python
import math

import jax
import jax.numpy as jnp
from jax import lax
from jax.sharding import PartitionSpec as P

HD = 64
EPS = 1e-06
BF = jnp.bfloat16
F32 = jnp.float32


def dot(a, b, dims):
    return lax.dot_general(a, b, (dims, ((), ())), preferred_element_type=F32)


def mm(a, b):
    return dot(a, b, ((1,), (0,)))


def mm_nt(a, b):
    return dot(a, b, ((1,), (1,)))


def mm_tn(a, b):
    return dot(a, b, ((0,), (0,)))


def core_swap(x):
    return lax.ppermute(x, "seq", [(i, i ^ 1) for i in range(lax.axis_size("seq"))])


def y_swap(x):
    return lax.ppermute(x, "seq", [(i, i ^ 2) for i in range(lax.axis_size("seq"))])


def shift(x, axis, distance):
    n = lax.axis_size(axis)
    return lax.ppermute(x, axis, [(i, (i + distance) % n) for i in range(n)])


def roll_blocks(pieces, index):
    n = len(pieces)
    ordered = [pieces[(n - m) % n] for m in range(n)]
    doubled = jnp.stack(ordered + ordered[: n - 1])
    return lax.dynamic_slice_in_dim(doubled, (n - index) % n, n, 0)


def place_blocks(pieces, index):
    n = len(pieces)
    out = jnp.zeros((n,) + pieces[0].shape, pieces[0].dtype)
    for k in range(n):
        out = lax.dynamic_update_slice_in_dim(out, pieces[k][None], (index - k + n) % n, 0)
    return out


def small(n):
    return n <= 8


def gather_small(x, axis):
    n = lax.axis_size(axis)
    if not small(n):
        return lax.all_gather(x, axis)
    pieces = [x] + [shift(x, axis, k) for k in range(1, n)]
    return roll_blocks(pieces, lax.axis_index(axis))


def scatter_sum_small(x, axis):
    n = lax.axis_size(axis)
    if not small(n):
        return lax.psum_scatter(x, axis, scatter_dimension=0, tiled=False)
    me = lax.axis_index(axis)
    total = lax.dynamic_index_in_dim(x, me, 0, keepdims=False)
    for k in range(1, n):
        block = lax.dynamic_index_in_dim(x, (me + k) % n, 0, keepdims=False)
        total = total + shift(block, axis, k)
    return total


def exchange_small(x, axis):
    n = lax.axis_size(axis)
    if not small(n):
        return lax.all_to_all(x, axis, split_axis=0, concat_axis=0, tiled=True)
    me = lax.axis_index(axis)
    pieces = []
    for k in range(n):
        block = lax.dynamic_index_in_dim(x, (me + k) % n, 0, keepdims=False)
        pieces.append(block if k == 0 else shift(block, axis, k))
    return roll_blocks(pieces, me)


def ring_gather(mine, other):
    n = lax.axis_size("fsdp")
    if not small(n):
        whole = lax.all_gather(mine, "fsdp")
        return whole, y_swap(whole)
    me = lax.axis_index("fsdp")
    mine_pieces = [mine]
    other_pieces = [other]
    for _ in range(n - 1):
        mine_pieces.append(shift(mine_pieces[-1], "fsdp", 1))
        other_pieces.append(y_swap(mine_pieces[-1]))
    return place_blocks(mine_pieces, me), place_blocks(other_pieces, me)


def ring_scatter(blocks):
    n = lax.axis_size("fsdp")
    if not small(n):
        return lax.psum_scatter(blocks.astype(BF), "fsdp", scatter_dimension=0, tiled=False).astype(F32)
    me = lax.axis_index("fsdp")
    acc = lax.dynamic_index_in_dim(blocks, (me + n - 1) % n, 0, keepdims=False).astype(F32)
    for k in range(2, n + 1):
        arrived = shift(acc.astype(BF), "fsdp", 1)
        own = lax.dynamic_index_in_dim(blocks, (me + n - k) % n, 0, keepdims=False)
        acc = own.astype(F32) + arrived.astype(F32)
    return acc


def embed_time(timestep, width):
    half = width // 2
    frequency = jnp.exp(-math.log(10000.0) * jnp.arange(half, dtype=F32) / half)
    angles = timestep.astype(F32)[:, None] * frequency[None, :]
    return jnp.concatenate([jnp.cos(angles), jnp.sin(angles)], axis=1)


def normalize(v):
    centered = v - jnp.mean(v, axis=-1, keepdims=True)
    inv_std = lax.rsqrt(jnp.mean(centered * centered, axis=-1, keepdims=True) + EPS)
    return centered * inv_std, inv_std


def normalize_back(u, normed, inv_std):
    return inv_std * (
        u
        - jnp.mean(u, axis=-1, keepdims=True)
        - normed * jnp.mean(u * normed, axis=-1, keepdims=True)
    )


def gelu(v):
    return jax.nn.gelu(v, approximate=True)


def swap_sum(partial):
    own = partial.astype(BF)
    return own.astype(F32) + core_swap(own).astype(F32)


def forward(h, mods, w):
    wqkv, wout, wup, wdown, low = w
    latents, tokens, width = h.shape
    rows = latents * tokens
    shift_one, scale_one, gate_one, shift_two, scale_two, gate_two = mods
    normed_one, rstd_one = normalize(h)
    attn_in = (normed_one * (1.0 + scale_one) + shift_one).astype(BF)
    flat_in = attn_in.reshape(rows, width)
    qkv = [mm(flat_in, part).astype(BF) for part in wqkv]
    heads = wqkv[0].shape[1] // 3 // HD

    def pick(i):
        got = [p.reshape(latents, tokens, 3, heads, HD)[:, :, i] for p in qkv]
        return jnp.concatenate(got, axis=2)

    q, k, v = pick(0), pick(1), pick(2)
    scores = jnp.einsum("lqhe,lkhe->lhqk", q, k, preferred_element_type=F32) * (1.0 / math.sqrt(HD))
    probs32 = jax.nn.softmax(scores, axis=-1)
    probs = probs32.astype(BF)
    att = jnp.einsum("lhqk,lkhe->lqhe", probs, v, preferred_element_type=F32).astype(BF)
    att = att.reshape(rows, 2 * heads * HD)
    att_other = core_swap(att)
    att_first = jnp.where(low == 0, att, att_other)
    att_second = jnp.where(low == 0, att_other, att)
    attended = jnp.concatenate([att_first, att_second], axis=1)
    projected = mm(attended, wout).reshape(h.shape)
    midway = h + gate_one * projected
    normed_two, rstd_two = normalize(midway)
    mlp_in = (normed_two * (1.0 + scale_two) + shift_two).astype(BF)
    flat_mlp = mlp_in.reshape(rows, width)
    pre = [mm(flat_mlp, part) for part in wup]
    hidden = [gelu(p).astype(BF) for p in pre]
    partial = mm(hidden[0], wdown[0]) + mm(hidden[1], wdown[1])
    mlp_out = swap_sum(partial).reshape(h.shape)
    out = midway + gate_two * mlp_out
    saved = (normed_one, rstd_one, flat_in, q, k, v, probs32, attended, projected,
             normed_two, rstd_two, flat_mlp, pre, hidden, mlp_out)
    return out, saved


def backward(g, saved, mods, w):
    wqkv, wout, wup, wdown, low = w
    (normed_one, rstd_one, flat_in, q, k, v, probs32, attended, projected,
     normed_two, rstd_two, flat_mlp, pre, hidden, mlp_out) = saved
    latents, tokens, width = g.shape
    rows = latents * tokens
    shift_one, scale_one, gate_one, shift_two, scale_two, gate_two = mods
    d_mlp = (gate_two * g).astype(BF).reshape(rows, width)
    d_gate_two = jnp.sum(g * mlp_out, axis=1)
    d_pre = [
        jax.vjp(gelu, p)[1](mm_nt(d_mlp, part))[0].astype(BF) for p, part in zip(pre, wdown)
    ]
    partial = mm_nt(d_pre[0], wup[0]) + mm_nt(d_pre[1], wup[1])
    d_mlp_in = swap_sum(partial).reshape(g.shape)
    d_shift_two = jnp.sum(d_mlp_in, axis=1)
    d_scale_two = jnp.sum(d_mlp_in * normed_two, axis=1)
    d_midway = g + normalize_back(d_mlp_in * (1.0 + scale_two), normed_two, rstd_two)
    d_proj = (gate_one * d_midway).astype(BF).reshape(rows, width)
    d_gate_one = jnp.sum(d_midway * projected, axis=1)
    half = wout.shape[0] // 2
    own_out = lax.dynamic_slice_in_dim(wout, low * half, half, 0)
    d_att = mm_nt(d_proj, own_out).astype(BF)
    heads = half // HD
    d_heads = d_att.reshape(latents, tokens, heads, HD)
    scale = 1.0 / math.sqrt(HD)
    d_probs = jnp.einsum("lqhe,lkhe->lhqk", d_heads, v, preferred_element_type=F32)
    delta = jnp.sum(probs32 * d_probs, axis=-1, keepdims=True)
    d_scores = (probs32 * (d_probs - delta)).astype(BF)
    dq = (jnp.einsum("lhqk,lkhe->lqhe", d_scores, k, preferred_element_type=F32) * scale).astype(BF)
    dk = (jnp.einsum("lhqk,lqhe->lkhe", d_scores, q, preferred_element_type=F32) * scale).astype(BF)
    dv = jnp.einsum(
        "lhqk,lqhe->lkhe", probs32.astype(BF), d_heads, preferred_element_type=F32
    ).astype(BF)
    stacked = jnp.stack([dq, dk, dv], axis=2).reshape(latents, tokens, 3, 2, heads // 2 * HD)
    d_qkv = [stacked[:, :, :, i].reshape(rows, 3 * heads // 2 * HD) for i in range(2)]
    partial = mm_nt(d_qkv[0], wqkv[0]) + mm_nt(d_qkv[1], wqkv[1])
    d_attn_in = swap_sum(partial).reshape(g.shape)
    d_shift_one = jnp.sum(d_attn_in, axis=1)
    d_scale_one = jnp.sum(d_attn_in * normed_one, axis=1)
    d_h = d_midway + normalize_back(d_attn_in * (1.0 + scale_one), normed_one, rstd_one)
    d_mod = jnp.concatenate(
        [d_shift_one, d_scale_one, d_gate_one, d_shift_two, d_scale_two, d_gate_two], axis=1
    )
    return d_h, d_mod, d_mlp, d_pre, d_proj, d_qkv


def body(boundary, timestep, label, label_table, ada_weight, qkv_weight, out_weight, up_weight, down_weight):
    on_first = lax.axis_index("section") == 0
    seq = lax.axis_index("seq")
    low, high = seq % 2, seq // 2
    fsdp = lax.axis_index("fsdp")
    n_seq, n_fsdp = lax.axis_size("seq"), lax.axis_size("fsdp")
    assert n_seq == 4
    width = boundary.shape[-1]
    tokens_here = boundary.shape[2]
    latents = boundary.shape[1] // 2
    ada, wqkv, wout, wup, wdown = (a[0] for a in (ada_weight, qkv_weight, out_weight, up_weight, down_weight))
    share = wqkv.shape[0]

    own = boundary[0]
    stay = lax.dynamic_slice_in_dim(own, high * latents, latents, 0)
    leave = lax.dynamic_slice_in_dim(own, (1 - high) * latents, latents, 0)
    half = jnp.concatenate([stay, y_swap(leave)], axis=1)
    half_other = core_swap(half)
    rows_in = jnp.concatenate(
        [jnp.where(low == 0, half, half_other), jnp.where(low == 0, half_other, half)], axis=1
    )
    own_rows = rows_in.astype(F32)

    cond = embed_time(timestep, width) + jnp.take(label_table, label, axis=0).astype(F32)
    silu_cond = jax.nn.silu(cond).astype(BF)
    silu_all = gather_small(silu_cond, "fsdp").reshape(-1, width)
    silu_cols = lax.dynamic_slice_in_dim(silu_all, fsdp * share, share, 1)
    partial_mod = mm(silu_cols, ada).reshape(n_fsdp, 2, latents, ada.shape[1])
    partial_mod = lax.dynamic_index_in_dim(partial_mod, high, 1, keepdims=False)
    modulation = scatter_sum_small(partial_mod, "fsdp")
    mods = [modulation[:, None, p * width : (p + 1) * width] for p in range(6)]

    def quarters(a, axis):
        return (
            lax.dynamic_index_in_dim(a, 2 * low + high, axis, keepdims=False),
            lax.dynamic_index_in_dim(a, 2 * low + 1 - high, axis, keepdims=False),
        )

    sub = wdown.shape[0] // 4
    qkv_parts = [p.reshape(share, -1) for p in quarters(wqkv.reshape(share, 3, 4, width // 4), 2)]
    out_parts = quarters(wout.reshape(share, 4, width // 4), 1)
    up_parts = [p.reshape(share, -1) for p in quarters(wup.reshape(share, n_fsdp, 4, sub), 2)]
    down_parts = quarters(wdown.reshape(4, sub, width), 0)
    gathered_qkv = [g.reshape(width, -1) for g in ring_gather(*qkv_parts)]
    gathered_out = ring_gather(*out_parts)
    gathered_up = [g.reshape(width, -1) for g in ring_gather(*up_parts)]
    gathered_down = [g.reshape(-1, width) for g in ring_gather(*down_parts)]
    out_here = jnp.where(
        high == 0,
        jnp.concatenate([g.reshape(width, -1) for g in gathered_out], axis=1),
        jnp.concatenate([g.reshape(width, -1) for g in gathered_out[::-1]], axis=1),
    )
    out_there = core_swap(out_here)
    out_full = jnp.where(
        low == 0,
        jnp.concatenate([out_here, out_there], axis=1),
        jnp.concatenate([out_there, out_here], axis=1),
    )
    by_heads = out_full.reshape(2, 2, width // 4, width)
    by_heads = jnp.where(high == 0, by_heads, by_heads[:, ::-1])
    out_full = by_heads.reshape(width, width)
    weights = (gathered_qkv, out_full, gathered_up, gathered_down, low)

    first_out, _ = forward(own_rows, mods, weights)
    n_sec = lax.axis_size("section")

    def cross(x, step):
        rows = x.astype(BF)
        half_tokens = rows.shape[1] // 2
        mine = lax.dynamic_slice_in_dim(rows, low * half_tokens, half_tokens, 1)
        route = [(i, i + step) for i in range(n_sec) if 0 <= i + step < n_sec]
        here = lax.ppermute(mine, "section", route)
        there = core_swap(here)
        return jnp.concatenate(
            [jnp.where(low == 0, here, there), jnp.where(low == 0, there, here)], axis=1
        ).astype(F32)

    passed = cross(first_out, 1)
    layer_in = jnp.where(on_first, own_rows, passed)
    layer_out, saved = forward(layer_in, mods, weights)

    second_back = backward(own_rows, saved, mods, weights)
    incoming = cross(second_back[0], -1)
    grad = jnp.where(on_first, incoming, own_rows)
    d_h, d_mod, d_mlp, d_pre, d_proj, d_qkv = backward(grad, saved, mods, weights)
    flat_in, attended, flat_mlp, hidden = saved[2], saved[7], saved[11], saved[13]

    def y_first(mine, other):
        total = mine + y_swap(other.astype(BF)).astype(F32)
        return ring_scatter(total.reshape((n_fsdp, -1) + total.shape[1:]))

    def y_last(mine, other):
        both = jnp.concatenate([mine, other], axis=1)
        here = ring_scatter(both.reshape((n_fsdp, -1) + both.shape[1:])).astype(BF)
        there = y_swap(here).astype(F32)
        cut = here.shape[1] // 2
        return here.astype(F32) + jnp.concatenate([there[:, cut:], there[:, :cut]], axis=1)

    def spread(by_part):
        ordered = jnp.where(high == 0, by_part, by_part[::-1])
        other = core_swap(ordered)
        return jnp.concatenate(
            [jnp.where(low == 0, ordered, other), jnp.where(low == 0, other, ordered)], axis=0
        )

    def from_y_first(total):
        mine = total.astype(BF)
        return spread(jnp.stack([mine, y_swap(mine)]))

    def from_y_last(total):
        cut = total.shape[1] // 2
        return spread(jnp.stack([total[:, :cut], total[:, cut:]]).astype(BF))

    g_down = from_y_first(y_first(mm_tn(hidden[0], d_mlp), mm_tn(hidden[1], d_mlp)))
    g_down = g_down.reshape(wdown.shape).astype(F32)
    g_up = from_y_first(y_first(mm_tn(flat_mlp, d_pre[0]), mm_tn(flat_mlp, d_pre[1])))
    g_up = g_up.reshape(4, share, n_fsdp, sub).transpose(1, 2, 0, 3).reshape(wup.shape).astype(F32)
    quarter = width // 4
    out_cols = [
        lax.dynamic_slice_in_dim(d_proj, (2 * low + part) * quarter, quarter, 1)
        for part in (high, 1 - high)
    ]
    att_order = attended.reshape(-1, 2, 2, quarter)
    att_order = jnp.where(high == 0, att_order, att_order[:, :, ::-1]).reshape(-1, width)
    g_out = from_y_last(y_last(mm_tn(att_order, out_cols[0]), mm_tn(att_order, out_cols[1])))
    g_out = g_out.transpose(1, 0, 2).reshape(wout.shape).astype(F32)
    g_qkv = from_y_last(y_last(mm_tn(flat_in, d_qkv[0]), mm_tn(flat_in, d_qkv[1])))
    g_qkv = g_qkv.reshape(4, share, 3, quarter).transpose(1, 2, 0, 3).reshape(wqkv.shape).astype(F32)

    d_mine = d_mod.astype(BF)
    d_there = y_swap(d_mine)
    d_six = jnp.concatenate(
        [jnp.where(high == 0, d_mine, d_there), jnp.where(high == 0, d_there, d_mine)], axis=0
    )
    d_all = gather_small(d_six, "fsdp").reshape(-1, d_six.shape[1])
    ada_cols = ada.shape[1] // n_seq
    g_ada = mm_tn(silu_cols, lax.dynamic_slice_in_dim(d_all, seq * ada_cols, ada_cols, 1))
    d_silu = mm_nt(d_all, ada).reshape(n_fsdp, 2 * latents, share)
    d_silu = exchange_small(d_silu, "fsdp").transpose(1, 0, 2).reshape(2 * latents, width)
    cond_grad = jax.vjp(jax.nn.silu, cond)[1](d_silu)[0]

    result = jnp.where(on_first, d_h, layer_out)
    blocks = result.reshape(latents, 2, 2, tokens_here, width)
    blocks = lax.dynamic_index_in_dim(blocks, low, 1, keepdims=False)
    keep = blocks[:, 0]
    arrive = y_swap(blocks[:, 1].astype(BF)).astype(F32)
    end_rows = jnp.where(
        high == 0, jnp.concatenate([keep, arrive], axis=0), jnp.concatenate([arrive, keep], axis=0)
    )
    return (
        end_rows[None],
        cond_grad[None],
        g_ada[None],
        g_qkv[None],
        g_out[None],
        g_up[None],
        g_down[None],
    )


def solution(mesh):
    rows = P("section", "fsdp", "seq", None)
    weight = P("section", "fsdp", None)
    return jax.shard_map(
        body,
        mesh=mesh,
        in_specs=(rows, P("fsdp"), P("fsdp"), P(), weight, weight, weight, weight, weight),
        out_specs=(rows, weight, P("section", "fsdp", "seq"), weight, weight, weight, weight),
        check_vma=False,
    )
```

time: 1820 us -> 641 us (0.35)
  waiting for transfers between devices: 910 us -> 162 us
  matrix products: 373 us -> 124 us
  blocking collectives: 211 us -> 0 us
  local copies, waits for them, and re-layouts: 136 us -> 184 us
    all_gather x5 -> x0, waiting for transfers between devices: 371 us -> none  [the longest x1 127 us: body(): lax.all_gather(ada_weight[0], 'fsdp', axis=0, tiled=True)]
    reduce_scatter x5 -> x0, waiting for transfers between devices: 339 us -> none  [the longest x1 165 us: body(): lax.psum_scatter(totals[2], 'fsdp', scatter_dimension=0, tiled=True)]
    dot_general x134 -> x46, matrix products: 373 us -> 119 us  [the longest x35 102 us: dot(): return lax.dot_general(a, b, (dims, ((), ())), preferred_element_type=F32)]
    all_to_all x21 -> x0, blocking collectives: 188 us -> none  [the longest x7 69.2 us: forward_layer(): lax.all_to_all(split_qkv, 'seq', split_axis=3, concat_axis=1, tiled=True)]
    psum x1 -> x0, waiting for transfers between devices: 136 us -> none  [body(): reduced = lax.psum((shares[1], shares[2], shares[3], shares[4]), 'seq')]
    ppermute x12 -> x75, waiting for transfers between devices: 34.9 us -> 162 us  [the longest x36 87.5 us: shift(): return lax.ppermute(x, axis, [(i, (i + distance) % n) for i in range(n)])]
    convert_element_type x0 -> x15, local copies, waits for them, and re-layouts: none -> 34.4 us  [the longest x3 15.3 us: body(): g_up.reshape(4, share, n_fsdp, sub).transpose(1, 2, 0, 3).reshape(wup.shape)]
    all_to_all x7 -> x0, starting transfers between devices: 27.3 us -> none  [the longest x4 16.1 us: backward_layer(): lax.all_to_all(stacked, 'seq', split_axis=1, concat_axis=3, tiled=True)]
  transfers between devices with their start and end apart: 30 -> 75, of which waited for: 26 -> 39; matrix products, arithmetic and copies ran while one was open for 13% -> 39% of each run, Pallas kernels for 0% -> 0%
where the time goes in v1:
time: 641 us; the launch traced here: 634 us
  local copies, waits for them, and re-layouts  184 us (29%)
  waiting for transfers between devices  162 us (25%)
  matrix products  124 us (19%)
  other arithmetic  99.9 us (16%)
  starting transfers between devices  60.2 us (9%)
    dot_general x35, matrix products, dot(): return lax.dot_general(a, b, (dims, ((), ())), preferred_element_type=F32)  102 us
    ppermute x36, waiting for transfers between devices, shift(): return lax.ppermute(x, axis, [(i, (i + distance) % n) for i in range(n)])  87.5 us
    ppermute x21, waiting for transfers between devices, y_swap(): lax.ppermute(x, 'seq', [(i, i ^ 2) for i in range(lax.axis_size('seq'))])  33.3 us
    ppermute x36, starting transfers between devices, shift(): return lax.ppermute(x, axis, [(i, (i + distance) % n) for i in range(n)])  31.5 us
    unnamed x262, local copies, waits for them, and re-layouts  29.4 us
    ppermute x2, waiting for transfers between devices, cross(): here = lax.ppermute(mine, 'section', route)  28.1 us
    dynamic_update_slice x31, local copies, waits for them, and re-layouts, place_blocks(): lax.dynamic_update_slice_in_dim(out, pieces[k][None], (index - k + n) % n...  26.7 us
    ppermute x21, starting transfers between devices, y_swap(): lax.ppermute(x, 'seq', [(i, i ^ 2) for i in range(lax.axis_size('seq'))])  21 us
  transfers between devices with their start and end apart: 75, of which 39 were waited for; matrix products, arithmetic and copies ran while one was open for 39% of the time, Pallas kernels for 0%

profile of v1, /device:TPU:0, one launch (start us, length us, event | category | flops | bytes accessed | tf_op | source)
XLA Modules:
  0.0 633.7 jit_solution(15599222745097336740)
XLA Ops:
  5.2 5.1 collective-permute-start.2
  33.8 4.5 reshape_squeeze.26
  38.3 6.1 dynamic-slice_reduce_fusion
  78.8 11.8 %collective-permute-done.16 = bf16[192,192]{1,0:T(8,128)(2,1)S(1)} collective-permute-done((bf16[192,192]{1,0:T(8,128)(2,1)S(1)}, bf16[192,192]{1,0:T(8,128)(2,1)S(1)}, u32[]{:S(2)}, u32[]{:S(2)}) %collective-permute-start.16) | collective-permute-done | bytes 73760 | tf_op jit(solution)/shard_map/ppermute | solution.py:40
  91.1 5.0 collective-permute-done.18
  97.8 3.9 collective-permute-done.19
  120.7 4.9 collective-permute-done.26
  127.8 3.1 collective-permute-done.23
  135.2 3.1 collective-permute-start.27
  152.0 6.7 %collective-permute-done.13 = bf16[192,576]{0,1:T(8,128)(2,1)S(1)} collective-permute-done((bf16[192,576]{0,1:T(8,128)(2,1)}, bf16[192,576]{0,1:T(8,128)(2,1)S(1)}, u32[]{:S(2)}, u32[]{:S(2)}) %collective-permute-start.13) | collective-permute-done | bytes 221216 | tf_op jit(solution)/shard_map/ppermute | solution.py:35
  163.1 3.0 convolution_convert_fusion.4
  166.1 3.1 reshape.1049
  172.5 3.0 convolution_convert_fusion.5
  175.5 3.1 reshape.1047
  181.4 3.6 fusion.178
  200.3 4.8 collective-permute-done.30
  214.5 5.6 fusion.59
  220.1 6.0 add_convert_fusion.11
  226.0 3.2 collective-permute-done.34
  231.3 4.4 collective-permute-start.35
  235.6 11.9 %collective-permute-done.35 = bf16[3,128,768]{2,1,0:T(8,128)(2,1)} collective-permute-done((bf16[3,128,768]{2,1,0:T(8,128)(2,1)S(1)}, bf16[3,128,768]{2,1,0:T(8,128)(2,1)}, u32[]{:S(2)}, u32[]{:S(2)}) %collective-permute-start.35) | collective-permute-done | bytes 589856 | tf_op jit(solution)/shard_map/ppermute | solution.py:308
  255.3 3.5 convolution_convert_fusion.2
  258.8 3.1 convolution_convert_fusion.3
  261.9 3.1 reshape.1062
  267.6 3.2 reshape.1061
  275.7 5.6 fusion.180
  281.2 3.1 fusion.57
  290.8 5.0 fusion.167
  297.2 4.2 fusion.189
  301.4 3.9 fusion.190
  305.3 7.1 %fusion.79 = f32[768,768]{1,0:T(8,128)} fusion(bf16[768,768]{1,0:T(8,128)(2,1)} %bitcast.48, f32[768,768]{1,0:T(8,128)} %fusion.189, bf16[768,768]{1,0:T(8,128)(2,1)} %bitcast.556, bf16[768,768]{1,0:T(8,128)(2,1)} %bitcast.54), kind=kOutput, calls=%fused_computation.184 | convolution fusion | flops 1823735808 | bytes 8257536 | tf_op jit(solution)/shard_map/dot_general | solution.py:15
  312.4 7.4 %add_convert_fusion.6 = bf16[768,768]{1,0:T(8,128)(2,1)} fusion(f32[768,768]{1,0:T(8,128)} %fusion.79, bf16[768,768]{1,0:T(8,128)(2,1)} %bitcast.58, f32[768,768]{1,0:T(8,128)} %fusion.190, bf16[768,768]{1,0:T(8,128)(2,1)} %bitcast.557, bf16[768,768]{1,0:T(8,128)(2,1)} %bitcast.549), kind=kOutput, calls=%fused_computation.97 | convolution fusion | flops 1824915456 | bytes 9437184 | tf_op jit(solution)/shard_map/dot_general | solution.py:15
  319.9 3.0 collective-permute-done.38
  326.5 4.1 multiply_convert_fusion.6
  336.1 3.7 multiply_reduce_fusion.1
  349.4 3.4 add_convert_fusion.5
  356.0 4.4 fusion.45
  360.5 3.1 fusion.61
  365.1 16.2 %collective-permute-done.40 = bf16[3,128,768]{2,1,0:T(8,128)(2,1)S(1)} collective-permute-done((bf16[3,128,768]{2,1,0:T(8,128)(2,1)}, bf16[3,128,768]{2,1,0:T(8,128)(2,1)S(1)}, u32[]{:S(2)}, u32[]{:S(2)}) %collective-permute-start.40) | collective-permute-done | bytes 589856 | tf_op jit(solution)/shard_map/ppermute | solution.py:308
  381.3 3.7 fusion.166
  390.7 3.5 add_convert_fusion.4
  417.2 4.7 multiply_reduce_fusion.6
  429.7 3.7 multiply_reduce_fusion
  444.8 3.4 add_convert_fusion.1
  450.2 5.2 copy.201
  466.3 3.5 convert_add_fusion.3
  470.2 4.4 collective-permute-done.58
  477.5 7.3 %collective-permute-done.59 = bf16[192,384]{1,0:T(8,128)(2,1)S(1)} collective-permute-done((bf16[192,384]{1,0:T(8,128)(2,1)S(1)}, bf16[192,384]{1,0:T(8,128)(2,1)S(1)}, u32[]{:S(2)}, u32[]{:S(2)}) %collective-permute-start.59) | collective-permute-done | bytes 147488 | tf_op jit(solution)/shard_map/ppermute | solution.py:40
  487.1 4.0 collective-permute-done.70
  491.3 3.0 collective-permute-done.60
  501.4 5.5 collective-permute-done.71
  511.8 11.1 %collective-permute-done.66 = bf16[192,768]{1,0:T(8,128)(2,1)} collective-permute-done((bf16[192,768]{1,0:T(8,128)(2,1)}, bf16[192,768]{1,0:T(8,128)(2,1)}, u32[]{:S(2)}, u32[]{:S(2)}) %collective-permute-start.66) | collective-permute-done | bytes 294944 | tf_op jit(solution)/shard_map/ppermute | solution.py:40
  533.8 3.6 collective-permute-done.73
  539.3 4.3 fusion.46
  548.0 5.8 multiply_reduce_fusion.7
  564.5 4.6 collective-permute-done.48
  569.6 5.7 collective-permute-done.49
  579.9 4.5 collective-permute-done.51
  585.5 4.6 collective-permute-done.52
  599.4 4.9 reshape.1089
  604.3 5.6 copy.279
  609.8 4.8 reshape.1086
  625.3 4.5 copy.203
  629.8 3.7 reshape.1084
  (630 shorter events, 318.1 us)
Async XLA Ops:
  5.2 51.5 %collective-permute-start.2 = (bf16[6,768]{1,0:T(8,128)(2,1)S(1)}, bf16[6,768]{1,0:T(8,128)(2,1)S(1)}, u32[]{:S(2)}, u32[]{:S(2)}) collective-permute-start(bf16[6,768]{1,0:T(8,128)(2,1)S(1)} %multiply_convert_fusion.7), channel_id=1, source_target_pairs={{0,3},{1,0},{2,1},{3,2},{4,7},{5,4},{6,5},{7,6},{8,11},{9,8},{10,9... | collective-permute-start | bytes 27656 | tf_op jit(solution)/shard_map/ppermute | solution.py:40
  10.3 47.0 %collective-permute-start.3 = (bf16[6,768]{1,0:T(8,128)(2,1)S(1)}, bf16[6,768]{1,0:T(8,128)(2,1)S(1)}, u32[]{:S(2)}, u32[]{:S(2)}) collective-permute-start(bf16[6,768]{1,0:T(8,128)(2,1)S(1)} %multiply_convert_fusion.7), channel_id=1, source_target_pairs={{0,2},{1,3},{2,0},{3,1},{4,6},{5,7},{6,4},{7,5},{8,10},{9,11},{10,... | collective-permute-start | bytes 27656 | tf_op jit(solution)/shard_map/ppermute | solution.py:40
  10.3 47.6 %collective-permute-start.4 = (bf16[6,768]{1,0:T(8,128)(2,1)S(1)}, bf16[6,768]{1,0:T(8,128)(2,1)S(1)}, u32[]{:S(2)}, u32[]{:S(2)}) collective-permute-start(bf16[6,768]{1,0:T(8,128)(2,1)S(1)} %multiply_convert_fusion.7), channel_id=1, source_target_pairs={{0,1},{1,2},{2,3},{3,0},{4,5},{5,6},{6,7},{7,4},{8,9},{9,10},{10,1... | collective-permute-start | bytes 27656 | tf_op jit(solution)/shard_map/ppermute | solution.py:40
  13.1 90.9 %collective-permute-start = (bf16[3,64,768]{2,1,0:T(8,128)(2,1)}, bf16[3,64,768]{2,1,0:T(8,128)(2,1)}, u32[]{:S(2)}, u32[]{:S(2)}) collective-permute-start(bf16[3,64,768]{2,1,0:T(8,128)(2,1)} %get-tuple-element.102), channel_id=1, source_target_pairs={{0,8},{4,12},{8,0},{12,4},{1,9},{5,13},{9,1},{13,5},{2,10},{6,14},... | collective-permute-start | bytes 884744 | tf_op jit(solution)/shard_map/ppermute | solution.py:35
  21.7 74.9 %collective-permute-start.8 = (bf16[192,576]{0,1:T(8,128)(2,1)}, bf16[192,576]{0,1:T(8,128)(2,1)}, u32[]{:S(2)}, u32[]{:S(2)}) collective-permute-start(bf16[192,576]{0,1:T(8,128)(2,1)} %bitcast.13), channel_id=1, source_target_pairs={{0,1},{1,2},{2,3},{3,0},{4,5},{5,6},{6,7},{7,4},{8,9},{9,10},{10,1... | collective-permute-start | bytes 663560 | tf_op jit(solution)/shard_map/ppermute | solution.py:40
  63.2 7.7 %collective-permute-start.7 = (f32[3,4608]{1,0:T(4,128)}, f32[3,4608]{1,0:T(4,128)}, u32[]{:S(2)}, u32[]{:S(2)}) collective-permute-start(f32[3,4608]{1,0:T(4,128)} %bitcast.452), channel_id=1, source_target_pairs={{0,3},{1,0},{2,1},{3,2},{4,7},{5,4},{6,5},{7,6},{8,11},{9,8},{10,9... | collective-permute-start | bytes 165896 | tf_op jit(solution)/shard_map/ppermute | solution.py:40
  65.2 7.6 %collective-permute-start.6 = (f32[3,4608]{1,0:T(4,128)}, f32[3,4608]{1,0:T(4,128)}, u32[]{:S(2)}, u32[]{:S(2)}) collective-permute-start(f32[3,4608]{1,0:T(4,128)} %bitcast.453), channel_id=1, source_target_pairs={{0,2},{1,3},{2,0},{3,1},{4,6},{5,7},{6,4},{7,5},{8,10},{9,11},{10,... | collective-permute-start | bytes 165896 | tf_op jit(solution)/shard_map/ppermute | solution.py:40
  66.0 7.5 %collective-permute-start.5 = (f32[3,4608]{1,0:T(4,128)}, f32[3,4608]{1,0:T(4,128)}, u32[]{:S(2)}, u32[]{:S(2)}) collective-permute-start(f32[3,4608]{1,0:T(4,128)} %bitcast.454), channel_id=1, source_target_pairs={{0,1},{1,2},{2,3},{3,0},{4,5},{5,6},{6,7},{7,4},{8,9},{9,10},{10,1... | collective-permute-start | bytes 165896 | tf_op jit(solution)/shard_map/ppermute | solution.py:40
  70.9 7.7 %collective-permute-start.15 = (bf16[192,192]{1,0:T(8,128)(2,1)}, bf16[192,192]{1,0:T(8,128)(2,1)S(1)}, u32[]{:S(2)}, u32[]{:S(2)}) collective-permute-start(bf16[192,192]{1,0:T(8,128)(2,1)} %bitcast.585), channel_id=1, source_target_pairs={{0,1},{1,2},{2,3},{3,0},{4,5},{5,6},{6,7},{7,4},{8,9},{9,10},{10,1... | collective-permute-start | bytes 221192 | tf_op jit(solution)/shard_map/ppermute | solution.py:40
  72.8 38.2 %collective-permute-start.25 = (bf16[192,768]{1,0:T(8,128)(2,1)}, bf16[192,768]{1,0:T(8,128)(2,1)}, u32[]{:S(2)}, u32[]{:S(2)}) collective-permute-start(bf16[192,768]{1,0:T(8,128)(2,1)} %get-tuple-element.86), channel_id=1, source_target_pairs={{0,1},{1,2},{2,3},{3,0},{4,5},{5,6},{6,7},{7,4},{8,9},{9,10},{10,1... | collective-permute-start | bytes 884744 | tf_op jit(solution)/shard_map/ppermute | solution.py:40
  73.5 39.7 %collective-permute-start.22 = (bf16[192,768]{1,0:T(8,128)(2,1)}, bf16[192,768]{1,0:T(8,128)(2,1)}, u32[]{:S(2)}, u32[]{:S(2)}) collective-permute-start(bf16[192,768]{1,0:T(8,128)(2,1)} %reshape.1055), channel_id=1, source_target_pairs={{0,1},{1,2},{2,3},{3,0},{4,5},{5,6},{6,7},{7,4},{8,9},{9,10},{10,1... | collective-permute-start | bytes 884744 | tf_op jit(solution)/shard_map/ppermute | solution.py:40
  78.6 11.9 %collective-permute-start.16 = (bf16[192,192]{1,0:T(8,128)(2,1)S(1)}, bf16[192,192]{1,0:T(8,128)(2,1)S(1)}, u32[]{:S(2)}, u32[]{:S(2)}) collective-permute-start(bf16[192,192]{1,0:T(8,128)(2,1)S(1)} %collective-permute-done.15), channel_id=1, source_target_pairs={{0,1},{1,2},{2,3},{3,0},{4,5},{5,6},{6,7},{7,4},{8,9},{9,10},{10,1... | collective-permute-start | bytes 221192 | tf_op jit(solution)/shard_map/ppermute | solution.py:40
  90.5 5.5 collective-permute-start.18
  96.1 5.6 collective-permute-start.19
  96.6 7.4 %collective-permute-start.17 = (bf16[192,192]{1,0:T(8,128)(2,1)S(1)}, bf16[192,192]{1,0:T(8,128)(2,1)S(1)}, u32[]{:S(2)}, u32[]{:S(2)}) collective-permute-start(bf16[192,192]{1,0:T(8,128)(2,1)S(1)} %collective-permute-done.16), channel_id=1, source_target_pairs={{0,1},{1,2},{2,3},{3,0},{4,5},{5,6},{6,7},{7,4},{8,9},{9,10},{10,1... | collective-permute-start | bytes 221192 | tf_op jit(solution)/shard_map/ppermute | solution.py:40
  101.7 14.9 %collective-permute-start.11 = (bf16[192,576]{0,1:T(8,128)(2,1)}, bf16[192,576]{0,1:T(8,128)(2,1)S(1)}, u32[]{:S(2)}, u32[]{:S(2)}) collective-permute-start(bf16[192,576]{0,1:T(8,128)(2,1)} %collective-permute-done.8), channel_id=1, source_target_pairs={{0,8},{4,12},{8,0},{12,4},{1,9},{5,13},{9,1},{13,5},{2,10},{6,14},... | collective-permute-start | bytes 663560 | tf_op jit(solution)/shard_map/ppermute | solution.py:35
  104.0 14.4 %collective-permute-start.9 = (bf16[192,576]{0,1:T(8,128)(2,1)}, bf16[192,576]{0,1:T(8,128)(2,1)S(1)}, u32[]{:S(2)}, u32[]{:S(2)}) collective-permute-start(bf16[192,576]{0,1:T(8,128)(2,1)} %collective-permute-done.8), channel_id=1, source_target_pairs={{0,1},{1,2},{2,3},{3,0},{4,5},{5,6},{6,7},{7,4},{8,9},{9,10},{10,1... | collective-permute-start | bytes 663560 | tf_op jit(solution)/shard_map/ppermute | solution.py:40
  104.1 5.6 collective-permute-start.20
  109.7 39.4 %collective-permute-start.1 = (bf16[3,128,768]{2,1,0:T(8,128)(2,1)}, bf16[3,128,768]{2,1,0:T(8,128)(2,1)}, u32[]{:S(2)}, u32[]{:S(2)}) collective-permute-start(bf16[3,128,768]{2,1,0:T(8,128)(2,1)} %pad_maximum_fusion.7), channel_id=1, source_target_pairs={{0,4},{4,0},{8,12},{12,8},{1,5},{5,1},{9,13},{13,9},{2,6},{6,2},{1... | collective-permute-start | bytes 1769480 | tf_op jit(solution)/shard_map/ppermute | solution.py:31
  111.0 75.3 %collective-permute-start.21 = (bf16[768,384]{1,0:T(8,128)(2,1)}, bf16[768,384]{1,0:T(8,128)(2,1)}, u32[]{:S(2)}, u32[]{:S(2)}) collective-permute-start(bf16[768,384]{1,0:T(8,128)(2,1)} %maximum_select_fusion.3), channel_id=1, source_target_pairs={{0,4},{4,0},{8,12},{12,8},{1,5},{5,1},{9,13},{13,9},{2,6},{6,2},{1... | collective-permute-start | bytes 1769480 | tf_op jit(solution)/shard_map/ppermute | solution.py:31
  113.2 12.4 %collective-permute-start.26 = (bf16[192,768]{1,0:T(8,128)(2,1)}, bf16[192,768]{1,0:T(8,128)(2,1)}, u32[]{:S(2)}, u32[]{:S(2)}) collective-permute-start(bf16[192,768]{1,0:T(8,128)(2,1)} %collective-permute-done.25), channel_id=1, source_target_pairs={{0,1},{1,2},{2,3},{3,0},{4,5},{5,6},{6,7},{7,4},{8,9},{9,10},{10,1... | collective-permute-start | bytes 884744 | tf_op jit(solution)/shard_map/ppermute | solution.py:40
  116.6 14.4 %collective-permute-start.23 = (bf16[192,768]{1,0:T(8,128)(2,1)}, bf16[192,768]{1,0:T(8,128)(2,1)}, u32[]{:S(2)}, u32[]{:S(2)}) collective-permute-start(bf16[192,768]{1,0:T(8,128)(2,1)} %collective-permute-done.22), channel_id=1, source_target_pairs={{0,1},{1,2},{2,3},{3,0},{4,5},{5,6},{6,7},{7,4},{8,9},{9,10},{10,1... | collective-permute-start | bytes 884744 | tf_op jit(solution)/shard_map/ppermute | solution.py:40
  118.5 15.0 %collective-permute-start.31 = (bf16[192,768]{1,0:T(8,128)(2,1)}, bf16[192,768]{1,0:T(8,128)(2,1)S(1)}, u32[]{:S(2)}, u32[]{:S(2)}) collective-permute-start(bf16[192,768]{1,0:T(8,128)(2,1)} %collective-permute-done.25), channel_id=1, source_target_pairs={{0,8},{4,12},{8,0},{12,4},{1,9},{5,13},{9,1},{13,5},{2,10},{6,14},... | collective-permute-start | bytes 884744 | tf_op jit(solution)/shard_map/ppermute | solution.py:35
  125.6 9.6 %collective-permute-start.28 = (bf16[192,768]{1,0:T(8,128)(2,1)}, bf16[192,768]{1,0:T(8,128)(2,1)S(1)}, u32[]{:S(2)}, u32[]{:S(2)}) collective-permute-start(bf16[192,768]{1,0:T(8,128)(2,1)} %collective-permute-done.22), channel_id=1, source_target_pairs={{0,8},{4,12},{8,0},{12,4},{1,9},{5,13},{9,1},{13,5},{2,10},{6,14},... | collective-permute-start | bytes 884744 | tf_op jit(solution)/shard_map/ppermute | solution.py:35
  131.0 9.3 %collective-permute-start.12 = (bf16[192,576]{0,1:T(8,128)(2,1)S(1)}, bf16[192,576]{0,1:T(8,128)(2,1)S(1)}, u32[]{:S(2)}, u32[]{:S(2)}) collective-permute-start(bf16[192,576]{0,1:T(8,128)(2,1)S(1)} %collective-permute-done.9), channel_id=1, source_target_pairs={{0,8},{4,12},{8,0},{12,4},{1,9},{5,13},{9,1},{13,5},{2,10},{6,14},... | collective-permute-start | bytes 663560 | tf_op jit(solution)/shard_map/ppermute | solution.py:35
  133.5 11.8 %collective-permute-start.10 = (bf16[192,576]{0,1:T(8,128)(2,1)S(1)}, bf16[192,576]{0,1:T(8,128)(2,1)}, u32[]{:S(2)}, u32[]{:S(2)}) collective-permute-start(bf16[192,576]{0,1:T(8,128)(2,1)S(1)} %collective-permute-done.9), channel_id=1, source_target_pairs={{0,1},{1,2},{2,3},{3,0},{4,5},{5,6},{6,7},{7,4},{8,9},{9,10},{10,1... | collective-permute-start | bytes 663560 | tf_op jit(solution)/shard_map/ppermute | solution.py:40
  135.2 54.3 %collective-permute-start.27 = (bf16[192,768]{1,0:T(8,128)(2,1)}, bf16[192,768]{1,0:T(8,128)(2,1)}, u32[]{:S(2)}, u32[]{:S(2)}) collective-permute-start(bf16[192,768]{1,0:T(8,128)(2,1)} %collective-permute-done.26), channel_id=1, source_target_pairs={{0,1},{1,2},{2,3},{3,0},{4,5},{5,6},{6,7},{7,4},{8,9},{9,10},{10,1... | collective-permute-start | bytes 884744 | tf_op jit(solution)/shard_map/ppermute | solution.py:40
  140.3 51.7 %collective-permute-start.24 = (bf16[192,768]{1,0:T(8,128)(2,1)}, bf16[192,768]{1,0:T(8,128)(2,1)}, u32[]{:S(2)}, u32[]{:S(2)}) collective-permute-start(bf16[192,768]{1,0:T(8,128)(2,1)} %collective-permute-done.23), channel_id=1, source_target_pairs={{0,1},{1,2},{2,3},{3,0},{4,5},{5,6},{6,7},{7,4},{8,9},{9,10},{10,1... | collective-permute-start | bytes 884744 | tf_op jit(solution)/shard_map/ppermute | solution.py:40
  145.4 49.7 %collective-permute-start.32 = (bf16[192,768]{1,0:T(8,128)(2,1)}, bf16[192,768]{1,0:T(8,128)(2,1)}, u32[]{:S(2)}, u32[]{:S(2)}) collective-permute-start(bf16[192,768]{1,0:T(8,128)(2,1)} %collective-permute-done.26), channel_id=1, source_target_pairs={{0,8},{4,12},{8,0},{12,4},{1,9},{5,13},{9,1},{13,5},{2,10},{6,14},... | collective-permute-start | bytes 884744 | tf_op jit(solution)/shard_map/ppermute | solution.py:35
  149.1 9.6 %collective-permute-start.13 = (bf16[192,576]{0,1:T(8,128)(2,1)}, bf16[192,576]{0,1:T(8,128)(2,1)S(1)}, u32[]{:S(2)}, u32[]{:S(2)}) collective-permute-start(bf16[192,576]{0,1:T(8,128)(2,1)} %collective-permute-done.10), channel_id=1, source_target_pairs={{0,8},{4,12},{8,0},{12,4},{1,9},{5,13},{9,1},{13,5},{2,10},{6,14},... | collective-permute-start | bytes 663560 | tf_op jit(solution)/shard_map/ppermute | solution.py:35
  158.7 38.1 %collective-permute-start.29 = (bf16[192,768]{1,0:T(8,128)(2,1)}, bf16[192,768]{1,0:T(8,128)(2,1)}, u32[]{:S(2)}, u32[]{:S(2)}) collective-permute-start(bf16[192,768]{1,0:T(8,128)(2,1)} %collective-permute-done.23), channel_id=1, source_target_pairs={{0,8},{4,12},{8,0},{12,4},{1,9},{5,13},{9,1},{13,5},{2,10},{6,14},... | collective-permute-start | bytes 884744 | tf_op jit(solution)/shard_map/ppermute | solution.py:35
  186.3 19.6 %collective-permute-start.14 = (bf16[768,384]{0,1:T(8,128)(2,1)S(1)}, bf16[768,384]{0,1:T(8,128)(2,1)S(1)}, u32[]{:S(2)}, u32[]{:S(2)}) collective-permute-start(bf16[768,384]{0,1:T(8,128)(2,1)S(1)} %bitcast.514), channel_id=1, source_target_pairs={{0,4},{4,0},{8,12},{12,8},{1,5},{5,1},{9,13},{13,9},{2,6},{6,2},{1... | collective-permute-start | bytes 1769480 | tf_op jit(solution)/shard_map/ppermute | solution.py:31
  189.6 10.1 %collective-permute-start.33 = (bf16[192,768]{1,0:T(8,128)(2,1)}, bf16[192,768]{1,0:T(8,128)(2,1)S(1)}, u32[]{:S(2)}, u32[]{:S(2)}) collective-permute-start(bf16[192,768]{1,0:T(8,128)(2,1)} %collective-permute-done.27), channel_id=1, source_target_pairs={{0,8},{4,12},{8,0},{12,4},{1,9},{5,13},{9,1},{13,5},{2,10},{6,14},... | collective-permute-start | bytes 884744 | tf_op jit(solution)/shard_map/ppermute | solution.py:35
  192.0 13.1 %collective-permute-start.30 = (bf16[192,768]{1,0:T(8,128)(2,1)}, bf16[192,768]{1,0:T(8,128)(2,1)S(1)}, u32[]{:S(2)}, u32[]{:S(2)}) collective-permute-start(bf16[192,768]{1,0:T(8,128)(2,1)} %collective-permute-done.24), channel_id=1, source_target_pairs={{0,8},{4,12},{8,0},{12,4},{1,9},{5,13},{9,1},{13,5},{2,10},{6,14},... | collective-permute-start | bytes 884744 | tf_op jit(solution)/shard_map/ppermute | solution.py:35
  231.3 16.3 %collective-permute-start.35 = (bf16[3,128,768]{2,1,0:T(8,128)(2,1)S(1)}, bf16[3,128,768]{2,1,0:T(8,128)(2,1)}, u32[]{:S(2)}, u32[]{:S(2)}) collective-permute-start(bf16[3,128,768]{2,1,0:T(8,128)(2,1)S(1)} %fusion.65), channel_id=1, source_target_pairs={{0,16},{1,17},{2,18},{3,19},{4,20},{5,21},{6,22},{7,23},{8,24},{9,... | collective-permute-start | bytes 1769480 | tf_op jit(solution)/shard_map/ppermute | solution.py:308
  363.6 17.7 %collective-permute-start.40 = (bf16[3,128,768]{2,1,0:T(8,128)(2,1)}, bf16[3,128,768]{2,1,0:T(8,128)(2,1)S(1)}, u32[]{:S(2)}, u32[]{:S(2)}) collective-permute-start(bf16[3,128,768]{2,1,0:T(8,128)(2,1)} %fusion.61), channel_id=1, source_target_pairs={{16,0},{17,1},{18,2},{19,3},{20,4},{21,5},{22,6},{23,7},{24,8},{25... | collective-permute-start | bytes 1769480 | tf_op jit(solution)/shard_map/ppermute | solution.py:308
  381.3 5.7 collective-permute-start.41
  386.6 17.3 %collective-permute-start.44 = (bf16[768,768]{1,0:T(8,128)(2,1)S(1)}, bf16[768,768]{1,0:T(8,128)(2,1)S(1)}, u32[]{:S(2)}, u32[]{:S(2)}) collective-permute-start(bf16[768,768]{1,0:T(8,128)(2,1)S(1)} %add_convert_fusion), channel_id=1, source_target_pairs={{0,4},{4,0},{8,12},{12,8},{1,5},{5,1},{9,13},{13,9},{2,6},{6,2},{1... | collective-permute-start | bytes 3538952 | tf_op jit(solution)/shard_map/ppermute | solution.py:31
  402.4 10.3 %collective-permute-start.42 = (bf16[768,768]{1,0:T(8,128)(2,1)S(1)}, bf16[768,768]{1,0:T(8,128)(2,1)S(1)}, u32[]{:S(2)}, u32[]{:S(2)}) collective-permute-start(bf16[768,768]{1,0:T(8,128)(2,1)S(1)} %add_convert_fusion.2), channel_id=1, source_target_pairs={{0,4},{4,0},{8,12},{12,8},{1,5},{5,1},{9,13},{13,9},{2,6},{6,2},{1... | collective-permute-start | bytes 3538952 | tf_op jit(solution)/shard_map/ppermute | solution.py:31
  407.9 58.4 %collective-permute-start.63 = (bf16[768,768]{1,0:T(8,128)(2,1)}, bf16[768,768]{1,0:T(8,128)(2,1)}, u32[]{:S(2)}, u32[]{:S(2)}) collective-permute-start(bf16[768,768]{1,0:T(8,128)(2,1)} %convolution_convert_fusion.1), channel_id=1, source_target_pairs={{0,8},{4,12},{8,0},{12,4},{1,9},{5,13},{9,1},{13,5},{2,10},{6,14},... | collective-permute-start | bytes 3538952 | tf_op jit(solution)/shard_map/ppermute | solution.py:35
  411.5 63.2 %collective-permute-start.69 = (bf16[768,768]{1,0:T(8,128)(2,1)}, bf16[768,768]{1,0:T(8,128)(2,1)}, u32[]{:S(2)}, u32[]{:S(2)}) collective-permute-start(bf16[768,768]{1,0:T(8,128)(2,1)} %convolution_convert_fusion), channel_id=1, source_target_pairs={{0,8},{4,12},{8,0},{12,4},{1,9},{5,13},{9,1},{13,5},{2,10},{6,14},... | collective-permute-start | bytes 3538952 | tf_op jit(solution)/shard_map/ppermute | solution.py:35
  448.2 91.1 %collective-permute-start.43 = (bf16[768,768]{1,0:T(8,128)(2,1)}, bf16[768,768]{1,0:T(8,128)(2,1)}, u32[]{:S(2)}, u32[]{:S(2)}) collective-permute-start(bf16[768,768]{1,0:T(8,128)(2,1)} %add_convert_fusion.1), channel_id=1, source_target_pairs={{0,4},{4,0},{8,12},{12,8},{1,5},{5,1},{9,13},{13,9},{2,6},{6,2},{1... | collective-permute-start | bytes 3538952 | tf_op jit(solution)/shard_map/ppermute | solution.py:31
  456.7 38.9 %collective-permute-start.53 = (bf16[192,1152]{1,0:T(8,128)(2,1)S(1)}, bf16[192,1152]{1,0:T(8,128)(2,1)}, u32[]{:S(2)}, u32[]{:S(2)}) collective-permute-start(bf16[192,1152]{1,0:T(8,128)(2,1)S(1)} %fusion.104), channel_id=1, source_target_pairs={{0,1},{1,2},{2,3},{3,0},{4,5},{5,6},{6,7},{7,4},{8,9},{9,10},{10,1... | collective-permute-start | bytes 1327112 | tf_op jit(solution)/shard_map/ppermute | solution.py:40
  465.5 9.1 %collective-permute-start.58 = (bf16[192,384]{1,0:T(8,128)(2,1)S(1)}, bf16[192,384]{1,0:T(8,128)(2,1)S(1)}, u32[]{:S(2)}, u32[]{:S(2)}) collective-permute-start(bf16[192,384]{1,0:T(8,128)(2,1)S(1)} %fusion.118), channel_id=1, source_target_pairs={{0,1},{1,2},{2,3},{3,0},{4,5},{5,6},{6,7},{7,4},{8,9},{9,10},{10,1... | collective-permute-start | bytes 442376 | tf_op jit(solution)/shard_map/ppermute | solution.py:40
  469.9 15.0 %collective-permute-start.64 = (bf16[192,768]{1,0:T(8,128)(2,1)S(1)}, bf16[192,768]{1,0:T(8,128)(2,1)S(1)}, u32[]{:S(2)}, u32[]{:S(2)}) collective-permute-start(bf16[192,768]{1,0:T(8,128)(2,1)S(1)} %fusion.109), channel_id=1, source_target_pairs={{0,1},{1,2},{2,3},{3,0},{4,5},{5,6},{6,7},{7,4},{8,9},{9,10},{10,1... | collective-permute-start | bytes 884744 | tf_op jit(solution)/shard_map/ppermute | solution.py:40
  474.6 10.2 %collective-permute-start.59 = (bf16[192,384]{1,0:T(8,128)(2,1)S(1)}, bf16[192,384]{1,0:T(8,128)(2,1)S(1)}, u32[]{:S(2)}, u32[]{:S(2)}) collective-permute-start(bf16[192,384]{1,0:T(8,128)(2,1)S(1)} %fusion.113), channel_id=1, source_target_pairs={{0,1},{1,2},{2,3},{3,0},{4,5},{5,6},{6,7},{7,4},{8,9},{9,10},{10,1... | collective-permute-start | bytes 442376 | tf_op jit(solution)/shard_map/ppermute | solution.py:40
  477.4 13.7 %collective-permute-start.70 = (bf16[192,768]{1,0:T(8,128)(2,1)S(1)}, bf16[192,768]{1,0:T(8,128)(2,1)S(1)}, u32[]{:S(2)}, u32[]{:S(2)}) collective-permute-start(bf16[192,768]{1,0:T(8,128)(2,1)S(1)} %fusion.110), channel_id=1, source_target_pairs={{0,1},{1,2},{2,3},{3,0},{4,5},{5,6},{6,7},{7,4},{8,9},{9,10},{10,1... | collective-permute-start | bytes 884744 | tf_op jit(solution)/shard_map/ppermute | solution.py:40
  484.9 9.4 %collective-permute-start.60 = (bf16[192,384]{1,0:T(8,128)(2,1)S(1)}, bf16[192,384]{1,0:T(8,128)(2,1)S(1)}, u32[]{:S(2)}, u32[]{:S(2)}) collective-permute-start(bf16[192,384]{1,0:T(8,128)(2,1)S(1)} %fusion.114), channel_id=1, source_target_pairs={{0,1},{1,2},{2,3},{3,0},{4,5},{5,6},{6,7},{7,4},{8,9},{9,10},{10,1... | collective-permute-start | bytes 442376 | tf_op jit(solution)/shard_map/ppermute | solution.py:40
  485.0 15.6 %collective-permute-start.65 = (bf16[192,768]{1,0:T(8,128)(2,1)S(1)}, bf16[192,768]{1,0:T(8,128)(2,1)S(1)}, u32[]{:S(2)}, u32[]{:S(2)}) collective-permute-start(bf16[192,768]{1,0:T(8,128)(2,1)S(1)} %fusion.97), channel_id=1, source_target_pairs={{0,1},{1,2},{2,3},{3,0},{4,5},{5,6},{6,7},{7,4},{8,9},{9,10},{10,1... | collective-permute-start | bytes 884744 | tf_op jit(solution)/shard_map/ppermute | solution.py:40
  491.2 15.7 %collective-permute-start.71 = (bf16[192,768]{1,0:T(8,128)(2,1)S(1)}, bf16[192,768]{1,0:T(8,128)(2,1)S(1)}, u32[]{:S(2)}, u32[]{:S(2)}) collective-permute-start(bf16[192,768]{1,0:T(8,128)(2,1)S(1)} %fusion.94), channel_id=1, source_target_pairs={{0,1},{1,2},{2,3},{3,0},{4,5},{5,6},{6,7},{7,4},{8,9},{9,10},{10,1... | collective-permute-start | bytes 884744 | tf_op jit(solution)/shard_map/ppermute | solution.py:40
  497.0 33.6 %collective-permute-start.54 = (bf16[192,1152]{1,0:T(8,128)(2,1)S(1)}, bf16[192,1152]{1,0:T(8,128)(2,1)}, u32[]{:S(2)}, u32[]{:S(2)}) collective-permute-start(bf16[192,1152]{1,0:T(8,128)(2,1)S(1)} %fusion.81), channel_id=1, source_target_pairs={{0,1},{1,2},{2,3},{3,0},{4,5},{5,6},{6,7},{7,4},{8,9},{9,10},{10,1... | collective-permute-start | bytes 1327112 | tf_op jit(solution)/shard_map/ppermute | solution.py:40
  500.0 7.8 %collective-permute-start.62 = (bf16[2,192,192]{2,1,0:T(8,128)(2,1)S(1)}, bf16[2,192,192]{2,1,0:T(8,128)(2,1)S(1)}, u32[]{:S(2)}, u32[]{:S(2)}) collective-permute-start(bf16[2,192,192]{2,1,0:T(8,128)(2,1)S(1)} %reverse_select_fusion.5), channel_id=1, source_target_pairs={{0,4},{4,0},{8,12},{12,8},{1,5},{5,1},{9,13},{13,9},{2,6},{6,2},{1... | collective-permute-start | bytes 442376 | tf_op jit(solution)/shard_map/ppermute | solution.py:31
  501.4 21.4 %collective-permute-start.66 = (bf16[192,768]{1,0:T(8,128)(2,1)}, bf16[192,768]{1,0:T(8,128)(2,1)}, u32[]{:S(2)}, u32[]{:S(2)}) collective-permute-start(bf16[192,768]{1,0:T(8,128)(2,1)} %fusion.98), channel_id=1, source_target_pairs={{0,1},{1,2},{2,3},{3,0},{4,5},{5,6},{6,7},{7,4},{8,9},{9,10},{10,1... | collective-permute-start | bytes 884744 | tf_op jit(solution)/shard_map/ppermute | solution.py:40
  507.8 20.3 %collective-permute-start.72 = (bf16[192,768]{1,0:T(8,128)(2,1)}, bf16[192,768]{1,0:T(8,128)(2,1)}, u32[]{:S(2)}, u32[]{:S(2)}) collective-permute-start(bf16[192,768]{1,0:T(8,128)(2,1)} %fusion.95), channel_id=1, source_target_pairs={{0,1},{1,2},{2,3},{3,0},{4,5},{5,6},{6,7},{7,4},{8,9},{9,10},{10,1... | collective-permute-start | bytes 884744 | tf_op jit(solution)/shard_map/ppermute | solution.py:40
  524.1 8.7 %collective-permute-start.67 = (bf16[192,768]{1,0:T(8,128)(2,1)S(1)}, bf16[192,768]{1,0:T(8,128)(2,1)S(1)}, u32[]{:S(2)}, u32[]{:S(2)}) collective-permute-start(bf16[192,768]{1,0:T(8,128)(2,1)S(1)} %fusion.99), channel_id=1, source_target_pairs={{0,8},{4,12},{8,0},{12,4},{1,9},{5,13},{9,1},{13,5},{2,10},{6,14},... | collective-permute-start | bytes 884744 | tf_op jit(solution)/shard_map/ppermute | solution.py:35
  529.3 8.0 %collective-permute-start.73 = (bf16[192,768]{1,0:T(8,128)(2,1)S(1)}, bf16[192,768]{1,0:T(8,128)(2,1)S(1)}, u32[]{:S(2)}, u32[]{:S(2)}) collective-permute-start(bf16[192,768]{1,0:T(8,128)(2,1)S(1)} %fusion.96), channel_id=1, source_target_pairs={{0,8},{4,12},{8,0},{12,4},{1,9},{5,13},{9,1},{13,5},{2,10},{6,14},... | collective-permute-start | bytes 884744 | tf_op jit(solution)/shard_map/ppermute | solution.py:35
  532.7 58.2 %collective-permute-start.55 = (bf16[192,1152]{1,0:T(8,128)(2,1)}, bf16[192,1152]{1,0:T(8,128)(2,1)}, u32[]{:S(2)}, u32[]{:S(2)}) collective-permute-start(bf16[192,1152]{1,0:T(8,128)(2,1)} %fusion.82), channel_id=1, source_target_pairs={{0,1},{1,2},{2,3},{3,0},{4,5},{5,6},{6,7},{7,4},{8,9},{9,10},{10,1... | collective-permute-start | bytes 1327112 | tf_op jit(solution)/shard_map/ppermute | solution.py:40
  533.8 62.7 %collective-permute-start.68 = (bf16[2,192,768]{2,1,0:T(8,128)(2,1)}, bf16[2,192,768]{2,1,0:T(8,128)(2,1)}, u32[]{:S(2)}, u32[]{:S(2)}) collective-permute-start(bf16[2,192,768]{2,1,0:T(8,128)(2,1)} %reverse_select_fusion.3), channel_id=1, source_target_pairs={{0,4},{4,0},{8,12},{12,8},{1,5},{5,1},{9,13},{13,9},{2,6},{6,2},{1... | collective-permute-start | bytes 1769480 | tf_op jit(solution)/shard_map/ppermute | solution.py:31
  539.2 75.5 %collective-permute-start.74 = (bf16[2,192,768]{2,1,0:T(8,128)(2,1)}, bf16[2,192,768]{2,1,0:T(8,128)(2,1)}, u32[]{:S(2)}, u32[]{:S(2)}) collective-permute-start(bf16[2,192,768]{2,1,0:T(8,128)(2,1)} %reverse_select_fusion.2), channel_id=1, source_target_pairs={{0,4},{4,0},{8,12},{12,8},{1,5},{5,1},{9,13},{13,9},{2,6},{6,2},{1... | collective-permute-start | bytes 1769480 | tf_op jit(solution)/shard_map/ppermute | solution.py:31
  556.6 37.8 %collective-permute-start.45 = (bf16[3,64,768]{2,1,0:T(8,128)(2,1)}, bf16[3,64,768]{2,1,0:T(8,128)(2,1)}, u32[]{:S(2)}, u32[]{:S(2)}) collective-permute-start(bf16[3,64,768]{2,1,0:T(8,128)(2,1)} %fusion.111), channel_id=1, source_target_pairs={{0,8},{4,12},{8,0},{12,4},{1,9},{5,13},{9,1},{13,5},{2,10},{6,14},... | collective-permute-start | bytes 884744 | tf_op jit(solution)/shard_map/ppermute | solution.py:35
  563.1 6.0 collective-permute-start.48
  569.1 6.2 collective-permute-start.49
  584.4 5.6 collective-permute-start.52
  593.2 22.8 %collective-permute-start.56 = (bf16[192,1152]{1,0:T(8,128)(2,1)}, bf16[192,1152]{1,0:T(8,128)(2,1)}, u32[]{:S(2)}, u32[]{:S(2)}) collective-permute-start(bf16[192,1152]{1,0:T(8,128)(2,1)} %fusion.83), channel_id=1, source_target_pairs={{0,8},{4,12},{8,0},{12,4},{1,9},{5,13},{9,1},{13,5},{2,10},{6,14},... | collective-permute-start | bytes 1327112 | tf_op jit(solution)/shard_map/ppermute | solution.py:35
  (118 other events, 1514.3 us)

commit v2 on v1

v2 whole, which is shorter than its diff:
```python
import math

import jax
import jax.numpy as jnp
from jax import lax
from jax.experimental import pallas as pl
from jax.experimental.pallas import tpu as pltpu
from jax.sharding import PartitionSpec as P

HD = 64
EPS = 1e-06
BF = jnp.bfloat16
F32 = jnp.float32


def dot(a, b, dims):
    return lax.dot_general(a, b, (dims, ((), ())), preferred_element_type=F32)


def mm(a, b):
    return dot(a, b, ((1,), (0,)))


def mm_nt(a, b):
    return dot(a, b, ((1,), (1,)))


def mm_tn(a, b):
    return dot(a, b, ((0,), (0,)))


def core_swap(x):
    return lax.ppermute(x, "seq", [(i, i ^ 1) for i in range(lax.axis_size("seq"))])


def y_swap(x):
    return lax.ppermute(x, "seq", [(i, i ^ 2) for i in range(lax.axis_size("seq"))])


def shift(x, axis, distance):
    n = lax.axis_size(axis)
    return lax.ppermute(x, axis, [(i, (i + distance) % n) for i in range(n)])


def roll_blocks(pieces, index):
    n = len(pieces)
    ordered = [pieces[(n - m) % n] for m in range(n)]
    doubled = jnp.stack(ordered + ordered[: n - 1])
    return lax.dynamic_slice_in_dim(doubled, (n - index) % n, n, 0)


def place_blocks(pieces, index):
    n = len(pieces)
    out = jnp.zeros((n,) + pieces[0].shape, pieces[0].dtype)
    for k in range(n):
        out = lax.dynamic_update_slice_in_dim(out, pieces[k][None], (index - k + n) % n, 0)
    return out


def small(n):
    return n <= 8


def gather_small(x, axis):
    n = lax.axis_size(axis)
    if not small(n):
        return lax.all_gather(x, axis)
    pieces = [x] + [shift(x, axis, k) for k in range(1, n)]
    return roll_blocks(pieces, lax.axis_index(axis))


def scatter_sum_small(x, axis):
    n = lax.axis_size(axis)
    if not small(n):
        return lax.psum_scatter(x, axis, scatter_dimension=0, tiled=False)
    me = lax.axis_index(axis)
    total = lax.dynamic_index_in_dim(x, me, 0, keepdims=False)
    for k in range(1, n):
        block = lax.dynamic_index_in_dim(x, (me + k) % n, 0, keepdims=False)
        total = total + shift(block, axis, k)
    return total


def exchange_small(x, axis):
    n = lax.axis_size(axis)
    if not small(n):
        return lax.all_to_all(x, axis, split_axis=0, concat_axis=0, tiled=True)
    me = lax.axis_index(axis)
    pieces = []
    for k in range(n):
        block = lax.dynamic_index_in_dim(x, (me + k) % n, 0, keepdims=False)
        pieces.append(block if k == 0 else shift(block, axis, k))
    return roll_blocks(pieces, me)


ANY = pl.BlockSpec(memory_space=pl.ANY)
SCALARS = pl.BlockSpec(memory_space=pltpu.SMEM)
VMEM = pl.BlockSpec(memory_space=pltpu.VMEM)


def params(mib=48):
    return pltpu.CompilerParams(vmem_limit_bytes=mib << 20)


def cost(flops, moved):
    return pl.CostEstimate(flops=int(flops), bytes_accessed=int(moved), transcendentals=0)


def sized(shape, dtype):
    return jax.ShapeDtypeStruct(shape, dtype)


def pick_kernel(blocks, block, place, w_ref, *refs):
    own_ref, mine_ref = refs[-2:]
    for b in range(blocks):
        start = pl.multiple_of((2 * b + place[0]) * block, 128)
        own_ref[:, b * block : (b + 1) * block] = w_ref[:, pl.ds(start, block)]
    half = mine_ref.shape[0]
    mine_ref[...] = own_ref[pl.ds(pl.multiple_of(place[1] * half, 16), half), :]


def pick_columns(w, blocks, place, after=()):
    rows, cols = w.shape
    block = cols // blocks // 2
    half = rows // 2
    if block % 128 or half % 16:
        own = lax.dynamic_index_in_dim(w.reshape(rows, blocks, 2, block), place[0], 2, keepdims=False)
        own = own.reshape(rows, blocks * block)
        return own, lax.dynamic_slice_in_dim(own, place[1] * half, half, 0)
    return pl.pallas_call(
        lambda *refs: pick_kernel(blocks, block, *refs),
        out_shape=(sized((rows, cols // 2), w.dtype), sized((half, cols // 2), w.dtype)),
        in_specs=[SCALARS, VMEM] + [ANY] * len(after),
        out_specs=(VMEM, VMEM),
        compiler_params=params(),
        cost_estimate=cost(0, 2 * rows * cols * 2),
    )(place, w, *after)


def assemble_kernel(n, share, place, own_ref, *refs):
    mine_refs, other_refs, out_ref, sems = refs[: n - 1], refs[n - 1 : 2 * n - 2], refs[-2], refs[-1]
    half = share // 2
    me = place[2]

    def rows(start, size):
        return out_ref.at[pl.ds(pl.multiple_of(start, 16), size)]

    copies = [pltpu.make_async_copy(own_ref, rows(me * share, share), sems.at[0])]
    for k in range(1, n):
        base = lax.rem(me - k + n, n) * share
        for j, (ref, part) in enumerate(((mine_refs[k - 1], place[1]), (other_refs[k - 1], 1 - place[1]))):
            copies.append(
                pltpu.make_async_copy(ref, rows(base + part * half, half), sems.at[2 * k - 1 + j])
            )
    for copy in copies:
        copy.start()
    for copy in copies:
        copy.wait()


def assemble(own, mine, other, place):
    n = len(mine) + 1
    share = own.shape[0]
    return pl.pallas_call(
        lambda *refs: assemble_kernel(n, share, *refs),
        out_shape=sized((n * share, own.shape[1]), own.dtype),
        in_specs=[SCALARS] + [ANY] * (2 * n - 1),
        out_specs=ANY,
        scratch_shapes=[pltpu.SemaphoreType.DMA((2 * n - 1,))],
        compiler_params=params(),
        cost_estimate=cost(0, 2 * n * share * own.shape[1] * 2),
    )(place, own, *mine, *other)


def ring_step_list(mine):
    n = lax.axis_size("fsdp")
    arrived, there = [], []
    block = mine
    for _ in range(n - 1):
        block = shift(block, "fsdp", 1)
        arrived.append(block)
        there.append(y_swap(block))
    return arrived, there


def whole_weight(own, mine, place):
    n = lax.axis_size("fsdp")
    if not small(n):
        here = lax.all_gather(mine, "fsdp")
        there = y_swap(here)
        pair = jnp.where(place[1] == 0, jnp.stack([here, there], 1), jnp.stack([there, here], 1))
        return pair.reshape(n * own.shape[0], own.shape[1]), here
    arrived, there = ring_step_list(mine)
    return assemble(own, arrived, there, place), arrived[-1]


def ring_scatter(blocks):
    n = lax.axis_size("fsdp")
    if not small(n):
        return lax.psum_scatter(blocks.astype(BF), "fsdp", scatter_dimension=0, tiled=False).astype(F32)
    me = lax.axis_index("fsdp")
    acc = lax.dynamic_index_in_dim(blocks, (me + n - 1) % n, 0, keepdims=False).astype(F32)
    for k in range(2, n + 1):
        arrived = shift(acc.astype(BF), "fsdp", 1)
        own = lax.dynamic_index_in_dim(blocks, (me + n - k) % n, 0, keepdims=False)
        acc = own.astype(F32) + arrived.astype(F32)
    return acc


def embed_time(timestep, width):
    half = width // 2
    frequency = jnp.exp(-math.log(10000.0) * jnp.arange(half, dtype=F32) / half)
    angles = timestep.astype(F32)[:, None] * frequency[None, :]
    return jnp.concatenate([jnp.cos(angles), jnp.sin(angles)], axis=1)


def normalize(v):
    centered = v - jnp.mean(v, axis=-1, keepdims=True)
    inv_std = lax.rsqrt(jnp.mean(centered * centered, axis=-1, keepdims=True) + EPS)
    return centered * inv_std, inv_std


def normalize_back(u, normed, inv_std):
    return inv_std * (
        u
        - jnp.mean(u, axis=-1, keepdims=True)
        - normed * jnp.mean(u * normed, axis=-1, keepdims=True)
    )


ROOT = math.sqrt(2.0 / math.pi)


def gelu(v):
    return 0.5 * v * (1.0 + jnp.tanh(ROOT * (v + 0.044715 * (v * v * v))))


def gelu_slope(v):
    t = jnp.tanh(ROOT * (v + 0.044715 * (v * v * v)))
    inner = ROOT * (1.0 + 3.0 * 0.044715 * (v * v))
    return 0.5 * (1.0 + t) + 0.5 * v * (1.0 - t * t) * inner


def lanes_of(shape, which):
    lane = lax.broadcasted_iota(jnp.int32, shape, 1)
    return (lane < HD) if which == 0 else (lane >= HD)


def softmax_rows(s):
    e = jnp.exp(s - jnp.max(s, axis=-1, keepdims=True))
    return e / jnp.sum(e, axis=-1, keepdims=True)


def keep_head(pair, which):
    return jnp.where(lanes_of(pair.shape, which), pair, jnp.zeros_like(pair))


def attend_kernel(h_ref, mod_ref, w_ref, qkv_ref, att_ref, in_ref=None):
    h = h_ref[0].astype(F32)
    normed, _ = normalize(h)
    x = (normed * (1.0 + mod_ref[0, 1:2, :]) + mod_ref[0, 0:1, :]).astype(BF)
    if in_ref is not None:
        in_ref[0] = x
    cols = w_ref.shape[1] // 3
    for part in range(3):
        qkv_ref[0, :, part * cols : (part + 1) * cols] = mm(
            x, w_ref[:, part * cols : (part + 1) * cols]
        ).astype(BF)
    for pair in range(cols // (2 * HD)):
        at = pair * 2 * HD
        q = qkv_ref[0, :, at : at + 2 * HD]
        k = qkv_ref[0, :, cols + at : cols + at + 2 * HD]
        v = qkv_ref[0, :, 2 * cols + at : 2 * cols + at + 2 * HD]
        total = None
        for which in range(2):
            s = mm_nt(keep_head(q, which), k) * (1.0 / math.sqrt(HD))
            o = mm(softmax_rows(s).astype(BF), keep_head(v, which))
            total = o if total is None else total + o
        att_ref[0, :, at : at + 2 * HD] = total.astype(BF)


def row_spec(tokens, width):
    return pl.BlockSpec((1, tokens, width), lambda i: (i, 0, 0))


def mod_spec(parts, width):
    return pl.BlockSpec((1, parts, width), lambda i: (i, 0, 0))


def attend(h, mods, wqkv, keep):
    latents, tokens, width = h.shape
    cols = wqkv.shape[1]
    outs = [(cols, BF), (cols // 3, BF)] + ([(width, BF)] if keep else [])
    return pl.pallas_call(
        attend_kernel,
        grid=(latents,),
        out_shape=tuple(sized((latents, tokens, c), t) for c, t in outs),
        in_specs=[row_spec(tokens, width), mod_spec(6, width), VMEM],
        out_specs=tuple(row_spec(tokens, c) for c, _ in outs),
        compiler_params=params(),
        cost_estimate=cost(latents * tokens * (2 * width * cols + 8 * tokens * cols), 8 << 20),
    )(h, mods, wqkv)


CHUNK = 512


def mlp_kernel(place, h_ref, mod_ref, own_ref, other_ref, wout_ref, wup_ref, wdown_ref,
               part_ref, midway_ref, proj_ref=None, in_ref=None, pre_ref=None, hidden_ref=None):
    half = own_ref.shape[2]
    low = place[0]
    projected = mm(own_ref[0], wout_ref[pl.ds(pl.multiple_of(low * half, 128), half), :])
    projected += mm(other_ref[0], wout_ref[pl.ds(pl.multiple_of((1 - low) * half, 128), half), :])
    midway = h_ref[0].astype(F32) + mod_ref[0, 2:3, :] * projected
    midway_ref[0] = midway
    normed, _ = normalize(midway)
    x = (normed * (1.0 + mod_ref[0, 4:5, :]) + mod_ref[0, 3:4, :]).astype(BF)
    if proj_ref is not None:
        proj_ref[0] = projected.astype(BF)
        in_ref[0] = x
    total = None
    for at in range(0, wup_ref.shape[1], CHUNK):
        pre = mm(x, wup_ref[:, at : at + CHUNK])
        hidden = gelu(pre).astype(BF)
        if pre_ref is not None:
            pre_ref[0, :, at : at + CHUNK] = pre
            hidden_ref[0, :, at : at + CHUNK] = hidden
        part = mm(hidden, wdown_ref[at : at + CHUNK, :])
        total = part if total is None else total + part
    part_ref[0] = total.astype(BF)


def mlp(place, h, mods, own, other, wout, wup, wdown, keep):
    latents, tokens, width = h.shape
    units = wup.shape[1]
    half = own.shape[2]
    outs = [(width, BF), (width, F32)]
    if keep:
        outs += [(width, BF), (width, BF), (units, F32), (units, BF)]
    return pl.pallas_call(
        mlp_kernel,
        grid=(latents,),
        out_shape=tuple(sized((latents, tokens, c), t) for c, t in outs),
        in_specs=[SCALARS, row_spec(tokens, width), mod_spec(6, width), row_spec(tokens, half),
                  row_spec(tokens, half), VMEM, VMEM, VMEM],
        out_specs=tuple(row_spec(tokens, c) for c, _ in outs),
        compiler_params=params(),
        cost_estimate=cost(latents * tokens * 2 * width * (2 * units + width), 16 << 20),
    )(place, h, mods, own, other, wout, wup, wdown)


def mlp_back_kernel(g_ref, mod_ref, pre_ref, wdown_ref, wup_ref, part_ref, d_pre_ref):
    d_mlp = (mod_ref[0, 5:6, :] * g_ref[0].astype(F32)).astype(BF)
    total = None
    for at in range(0, wup_ref.shape[1], CHUNK):
        d_hidden = mm_nt(d_mlp, wdown_ref[at : at + CHUNK, :])
        d_pre = (d_hidden * gelu_slope(pre_ref[0, :, at : at + CHUNK])).astype(BF)
        d_pre_ref[0, :, at : at + CHUNK] = d_pre
        part = mm_nt(d_pre, wup_ref[:, at : at + CHUNK])
        total = part if total is None else total + part
    part_ref[0] = total.astype(BF)


def mlp_back(g, mods, pre, wdown, wup):
    latents, tokens, width = g.shape
    units = wup.shape[1]
    return pl.pallas_call(
        mlp_back_kernel,
        grid=(latents,),
        out_shape=(sized((latents, tokens, width), BF), sized((latents, tokens, units), BF)),
        in_specs=[row_spec(tokens, width), mod_spec(6, width), row_spec(tokens, units), VMEM, VMEM],
        out_specs=(row_spec(tokens, width), row_spec(tokens, units)),
        compiler_params=params(),
        cost_estimate=cost(latents * tokens * 4 * width * units, 14 << 20),
    )(g, mods, pre, wdown, wup)


def attend_back_kernel(place, own_ref, other_ref, g_ref, midway_ref, proj_ref, mod_ref, qkv_ref,
                       wout_ref, wqkv_ref, part_ref, d_mid_ref, d_proj_ref, d_qkv_ref, sums_ref):
    d_in = own_ref[0].astype(F32) + other_ref[0].astype(F32)
    normed, inv_std = normalize(midway_ref[0])
    sums_ref[0, 1:2, :] = jnp.sum(d_in, axis=0, keepdims=True)
    sums_ref[0, 2:3, :] = jnp.sum(d_in * normed, axis=0, keepdims=True)
    d_mid = g_ref[0].astype(F32) + normalize_back(d_in * (1.0 + mod_ref[0, 4:5, :]), normed, inv_std)
    d_mid_ref[0] = d_mid
    d_proj = (mod_ref[0, 2:3, :] * d_mid).astype(BF)
    d_proj_ref[0] = d_proj
    sums_ref[0, 0:1, :] = jnp.sum(d_mid * proj_ref[0].astype(F32), axis=0, keepdims=True)
    cols = wqkv_ref.shape[1] // 3
    low = place[0]
    d_att = mm_nt(d_proj, wout_ref[pl.ds(pl.multiple_of(low * cols, 128), cols), :]).astype(BF)
    scale = 1.0 / math.sqrt(HD)
    for pair in range(cols // (2 * HD)):
        at = pair * 2 * HD
        q = qkv_ref[0, :, at : at + 2 * HD]
        k = qkv_ref[0, :, cols + at : cols + at + 2 * HD]
        v = qkv_ref[0, :, 2 * cols + at : 2 * cols + at + 2 * HD]
        d_o = d_att[:, at : at + 2 * HD]
        dq = dk = dv = 0.0
        for which in range(2):
            q_one, d_one = keep_head(q, which), keep_head(d_o, which)
            probs = softmax_rows(mm_nt(q_one, k) * scale)
            d_probs = mm_nt(d_one, v)
            delta = jnp.sum(probs * d_probs, axis=-1, keepdims=True)
            d_s = (probs * (d_probs - delta)).astype(BF)
            dq += mm(d_s, keep_head(k, which))
            dk += mm_tn(d_s, q_one)
            dv += mm_tn(probs.astype(BF), d_one)
        d_qkv_ref[0, :, at : at + 2 * HD] = (dq * scale).astype(BF)
        d_qkv_ref[0, :, cols + at : cols + at + 2 * HD] = (dk * scale).astype(BF)
        d_qkv_ref[0, :, 2 * cols + at : 2 * cols + at + 2 * HD] = dv.astype(BF)
    part_ref[0] = mm_nt(d_qkv_ref[0], wqkv_ref[...]).astype(BF)


def attend_back(place, own, other, g, midway, projected, mods, qkv, wout, wqkv):
    latents, tokens, width = g.shape
    cols = wqkv.shape[1]
    rows = row_spec(tokens, width)
    return pl.pallas_call(
        attend_back_kernel,
        grid=(latents,),
        out_shape=(
            sized(g.shape, BF),
            sized(g.shape, F32),
            sized(g.shape, BF),
            sized((latents, tokens, cols), BF),
            sized((latents, 3, width), F32),
        ),
        in_specs=[SCALARS, rows, rows, rows, rows, rows, mod_spec(6, width), row_spec(tokens, cols), VMEM, VMEM],
        out_specs=(rows, rows, rows, row_spec(tokens, cols), mod_spec(3, width)),
        compiler_params=params(),
        cost_estimate=cost(latents * tokens * (2 * width * cols + 20 * tokens * cols), 14 << 20),
    )(place, own, other, g, midway, projected, mods, qkv, wout, wqkv)


def inputs_back_kernel(own_ref, other_ref, h_ref, d_mid_ref, mod_ref, d_h_ref, sums_ref):
    d_in = own_ref[0].astype(F32) + other_ref[0].astype(F32)
    normed, inv_std = normalize(h_ref[0].astype(F32))
    sums_ref[0, 0:1, :] = jnp.sum(d_in, axis=0, keepdims=True)
    sums_ref[0, 1:2, :] = jnp.sum(d_in * normed, axis=0, keepdims=True)
    d_h = d_mid_ref[0] + normalize_back(d_in * (1.0 + mod_ref[0, 1:2, :]), normed, inv_std)
    d_h_ref[0] = d_h.astype(d_h_ref.dtype)


def inputs_back(own, other, h, d_mid, mods, dtype):
    latents, tokens, width = h.shape
    rows = row_spec(tokens, width)
    return pl.pallas_call(
        inputs_back_kernel,
        grid=(latents,),
        out_shape=(sized(h.shape, dtype), sized((latents, 2, width), F32)),
        in_specs=[rows, rows, rows, rows, mod_spec(6, width)],
        out_specs=(rows, mod_spec(2, width)),
        compiler_params=params(),
        cost_estimate=cost(0, 10 << 20),
    )(own, other, h, d_mid, mods)


def body(boundary, timestep, label, label_table, ada_weight, qkv_weight, out_weight, up_weight, down_weight):
    on_first = lax.axis_index("section") == 0
    seq = lax.axis_index("seq")
    low, high = seq % 2, seq // 2
    fsdp = lax.axis_index("fsdp")
    n_seq, n_fsdp, n_sec = lax.axis_size("seq"), lax.axis_size("fsdp"), lax.axis_size("section")
    assert n_seq == 4
    place = jnp.stack([low, high, fsdp]).astype(jnp.int32)
    width = boundary.shape[-1]
    tokens_here = boundary.shape[2]
    latents = boundary.shape[1] // 2
    ada, wqkv, wout, wup, wdown = (a[0] for a in (ada_weight, qkv_weight, out_weight, up_weight, down_weight))
    share = wqkv.shape[0]

    def by_core(here, there):
        return jnp.where(low == 0, here, there), jnp.where(low == 0, there, here)

    qkv_own, qkv_mine = pick_columns(wqkv, 3, place)
    full_qkv, token = whole_weight(qkv_own, qkv_mine, place)

    own = boundary[0]
    stay = lax.dynamic_slice_in_dim(own, high * latents, latents, 0)
    leave = lax.dynamic_slice_in_dim(own, (1 - high) * latents, latents, 0)
    half = jnp.concatenate([stay, y_swap(leave)], axis=1)
    own_rows = jnp.concatenate(by_core(half, core_swap(half)), axis=1)

    cond = embed_time(timestep, width) + jnp.take(label_table, label, axis=0).astype(F32)
    silu_cond = jax.nn.silu(cond).astype(BF)
    silu_all = gather_small(silu_cond, "fsdp").reshape(-1, width)
    silu_cols = lax.dynamic_slice_in_dim(silu_all, fsdp * share, share, 1)
    partial_mod = mm(silu_cols, ada).reshape(n_fsdp, 2, latents, ada.shape[1])
    partial_mod = lax.dynamic_index_in_dim(partial_mod, high, 1, keepdims=False)
    modulation = scatter_sum_small(partial_mod, "fsdp")
    mods = modulation.reshape(latents, 6, width)

    quarter = share // 4
    out_own = lax.dynamic_slice_in_dim(wout, (2 * high + low) * quarter, quarter, 0)
    if small(n_fsdp):
        out_arrived, out_there = ring_step_list(out_own)
        out_two = jnp.stack([jnp.stack(out_arrived), jnp.stack(out_there)], 1)
        out_two = jnp.where(high == 0, out_two, out_two[:, ::-1])
        out_four = jnp.stack(by_core(out_two, core_swap(out_two)), 2)
        pieces = [wout] + [out_four[k].reshape(share, width) for k in range(n_fsdp - 1)]
        full_out = place_blocks(pieces, fsdp).reshape(-1, width)
    else:
        full_out = lax.all_gather(wout, "fsdp", axis=0, tiled=True)
    up_own, up_mine = pick_columns(wup, n_fsdp, place, (token,))
    full_up, _ = whole_weight(up_own, up_mine, place)
    sub = wdown.shape[0] // 2
    down_own = lax.dynamic_slice_in_dim(wdown, low * sub, sub, 0)
    down_mine = lax.dynamic_slice_in_dim(down_own, high * (sub // 2), sub // 2, 0)
    full_down, _ = whole_weight(down_own, down_mine, place)

    def cross(rows, step):
        half_tokens = rows.shape[1] // 2
        mine = lax.dynamic_slice_in_dim(rows, low * half_tokens, half_tokens, 1)
        route = [(i, i + step) for i in range(n_sec) if 0 <= i + step < n_sec]
        here = lax.ppermute(mine, "section", route)
        return jnp.concatenate(by_core(here, core_swap(here)), axis=1)

    gate_two = mods[:, 5:6]

    _, att = attend(own_rows, mods, full_qkv, False)
    part, midway = mlp(place, own_rows, mods, att, core_swap(att), full_out, full_up, full_down, False)
    mlp_out = part.astype(F32) + core_swap(part).astype(F32)
    passed = cross((midway + gate_two * mlp_out).astype(BF), 1)

    h = jnp.where(on_first, own_rows, passed)
    qkv, att, attn_in = attend(h, mods, full_qkv, True)
    att_other = core_swap(att)
    part, midway, projected, mlp_in, pre, hidden = mlp(
        place, h, mods, att, att_other, full_out, full_up, full_down, True
    )
    mlp_out = part.astype(F32) + core_swap(part).astype(F32)
    layer_out = midway + gate_two * mlp_out

    def backward(g, dtype):
        part, d_pre = mlp_back(g, mods, pre, full_down, full_up)
        part_two, d_mid, d_proj, d_qkv, sums_mid = attend_back(
            place, part, core_swap(part), g, midway, projected, mods, qkv, full_out, full_qkv
        )
        d_h, sums_in = inputs_back(part_two, core_swap(part_two), h, d_mid, mods, dtype)
        return d_h, d_pre, d_proj, d_qkv, sums_mid, sums_in

    incoming = cross(backward(own_rows, BF)[0], -1)
    g = jnp.where(on_first, incoming, own_rows)
    d_mlp = (gate_two * g.astype(F32)).astype(BF)
    d_gate_two = jnp.sum(g.astype(F32) * mlp_out, axis=1)
    d_h, d_pre, d_proj, d_qkv, sums_mid, sums_in = backward(g, F32)

    def flat(a):
        return a.reshape(-1, a.shape[-1])

    def halves(a):
        split = a.reshape(n_fsdp, 2, -1, a.shape[-1])
        return (
            lax.dynamic_index_in_dim(split, high, 1, keepdims=False),
            lax.dynamic_index_in_dim(split, 1 - high, 1, keepdims=False),
        )

    def y_first(a):
        mine, other = halves(a)
        total = ring_scatter(mine.astype(F32) + y_swap(other.astype(BF)).astype(F32)).astype(BF)
        there = y_swap(total)
        return jnp.where(
            high == 0, jnp.concatenate([total, there]), jnp.concatenate([there, total])
        )

    def y_last(a):
        here = ring_scatter(a.reshape(n_fsdp, -1, a.shape[-1])).astype(BF)
        return (here.astype(F32) + y_swap(here).astype(F32)).astype(BF)

    def both_cores(a, blocks):
        rows = a.shape[0]
        pair = [p.reshape(rows, blocks, -1) for p in by_core(a, core_swap(a))]
        return jnp.stack(pair, 2).reshape(rows, -1).astype(F32)

    g_down = y_first(mm_tn(flat(hidden), flat(d_mlp)))
    g_down = jnp.concatenate(by_core(g_down, core_swap(g_down))).astype(F32)
    g_up = both_cores(y_first(mm_tn(flat(mlp_in), flat(d_pre))), n_fsdp)
    cols = width // 2
    own_cols = lax.dynamic_slice_in_dim(flat(d_proj), low * cols, cols, 1)
    attended = jnp.concatenate(by_core(flat(att), flat(att_other)), axis=1)
    g_out = both_cores(y_last(mm_tn(attended, own_cols)), 1)
    g_qkv = both_cores(y_last(mm_tn(flat(attn_in), flat(d_qkv))), 3)

    d_mod = jnp.concatenate([flat_sums.reshape(latents, -1) for flat_sums in (sums_in, sums_mid, d_gate_two)], axis=1)
    d_mine = d_mod.astype(BF)
    d_there = y_swap(d_mine)
    d_six = jnp.where(
        high == 0, jnp.concatenate([d_mine, d_there]), jnp.concatenate([d_there, d_mine])
    )
    d_all = gather_small(d_six, "fsdp").reshape(-1, d_six.shape[1])
    ada_cols = ada.shape[1] // n_seq
    g_ada = mm_tn(silu_cols, lax.dynamic_slice_in_dim(d_all, seq * ada_cols, ada_cols, 1))
    d_silu = mm_nt(d_all, ada).reshape(n_fsdp, 2 * latents, share)
    d_silu = exchange_small(d_silu, "fsdp").transpose(1, 0, 2).reshape(2 * latents, width)
    cond_grad = jax.vjp(jax.nn.silu, cond)[1](d_silu)[0]

    result = jnp.where(on_first, d_h, layer_out)
    blocks = result.reshape(latents, 2, 2, tokens_here, width)
    blocks = lax.dynamic_index_in_dim(blocks, low, 1, keepdims=False)
    keep = blocks[:, 0]
    arrive = y_swap(blocks[:, 1].astype(BF)).astype(F32)
    end_rows = jnp.where(
        high == 0, jnp.concatenate([keep, arrive], axis=0), jnp.concatenate([arrive, keep], axis=0)
    )
    return (
        end_rows[None],
        cond_grad[None],
        g_ada[None],
        g_qkv[None],
        g_out[None],
        g_up[None],
        g_down[None],
    )


def solution(mesh):
    rows = P("section", "fsdp", "seq", None)
    weight = P("section", "fsdp", None)
    return jax.shard_map(
        body,
        mesh=mesh,
        in_specs=(rows, P("fsdp"), P("fsdp"), P(), weight, weight, weight, weight, weight),
        out_specs=(rows, weight, P("section", "fsdp", "seq"), weight, weight, weight, weight),
        check_vma=False,
    )
```

time: 641 us -> 478 us (0.75)
  local copies, waits for them, and re-layouts: 184 us -> 59.9 us
  matrix products: 124 us -> 8.66 us
  Pallas kernels: 0 us -> 103 us
  other arithmetic: 99.9 us -> 40.2 us
  waiting for transfers between devices: 162 us -> 202 us
  starting transfers between devices: 60.2 us -> 52.1 us
    pallas_call x0 -> x15, Pallas kernels: none -> 103 us  [the longest x2 30.9 us: attend_back(): pl.pallas_call(attend_back_kernel, grid=(latents,), out_shape=(sized(g.sh...]
    dot_general x35 -> x7, matrix products: 102 us -> 8.66 us  [dot(): return lax.dot_general(a, b, (dims, ((), ())), preferred_element_type=F32)]
    ppermute x21, waiting for transfers between devices: 33.3 us -> 62 us  [y_swap(): lax.ppermute(x, 'seq', [(i, i ^ 2) for i in range(lax.axis_size('seq'))])]
    dynamic_update_slice x31 -> x4, local copies, waits for them, and re-layouts: 26.7 us -> 0.1 us  [place_blocks(): lax.dynamic_update_slice_in_dim(out, pieces[k][None], (index - k + n) % n...]
    reduce_sum x14 -> x1, other arithmetic: 27.3 us -> 2.05 us  [body(): d_gate_two = jnp.sum(g.astype(F32) * mlp_out, axis=1)]
    reshape x9 -> x1, local copies, waits for them, and re-layouts: 22.6 us -> 1.55 us  [body(): mods = modulation.reshape(latents, 6, width)]
    another operation x19 -> x8, local copies, waits for them, and re-layouts: 21.4 us -> 0.76 us  [both_cores(): return jnp.stack(pair, 2).reshape(rows, -1).astype(F32)]
    dot_general x11 -> x0, matrix products: 16.3 us -> none  [the longest x2 7.48 us: backward(): jnp.einsum('lqhe,lkhe->lhqk', d_heads, v, preferred_element_type=F32)]
  transfers between devices with their start and end apart: 75 -> 75, of which waited for: 39 -> 39; matrix products, arithmetic and copies ran while one was open for 39% -> 16% of each run, Pallas kernels for 0% -> 9%
where the time goes in v2:
time: 478 us; the launch traced here: 469 us
  waiting for transfers between devices  202 us (42%)
  Pallas kernels  103 us (22%)
  local copies, waits for them, and re-layouts  59.9 us (13%)
  starting transfers between devices  52.1 us (11%)
  other arithmetic  40.2 us (8%)
  matrix products  8.66 us (2%)
    ppermute x36, waiting for transfers between devices, shift(): return lax.ppermute(x, axis, [(i, (i + distance) % n) for i in range(n)])  99.8 us
    ppermute x21, waiting for transfers between devices, y_swap(): lax.ppermute(x, 'seq', [(i, i ^ 2) for i in range(lax.axis_size('seq'))])  62 us
    pallas_call x2, Pallas kernels, attend_back(): pl.pallas_call(attend_back_kernel, grid=(latents,), out_shape=(sized(g.sh...  30.9 us
    ppermute x2, waiting for transfers between devices, cross(): here = lax.ppermute(mine, 'section', route)  28.4 us
    ppermute x36, starting transfers between devices, shift(): return lax.ppermute(x, axis, [(i, (i + distance) % n) for i in range(n)])  25.2 us
    pallas_call x2, Pallas kernels, mlp(): pl.pallas_call(mlp_kernel, grid=(latents,), out_shape=tuple((sized((laten...  23.3 us
    ppermute x21, starting transfers between devices, y_swap(): lax.ppermute(x, 'seq', [(i, i ^ 2) for i in range(lax.axis_size('seq'))])  20.5 us
    unnamed x130, local copies, waits for them, and re-layouts  20.2 us
  transfers between devices with their start and end apart: 75, of which 39 were waited for; matrix products, arithmetic and copies ran while one was open for 16% of the time, Pallas kernels for 9%

profile of v2, /device:TPU:0, one launch (start us, length us, event | category | flops | bytes accessed | tf_op | source)
XLA Modules:
  0.0 468.7 jit_solution(12795640387187712151)
XLA Ops:
  2.9 2.2 gather_fusion
  5.2 5.1 %collective-permute-start.2 = (bf16[6,768]{1,0:T(8,128)(2,1)S(1)}, bf16[6,768]{1,0:T(8,128)(2,1)S(1)}, u32[]{:S(2)}, u32[]{:S(2)}) collective-permute-start(bf16[6,768]{1,0:T(8,128)(2,1)S(1)} %multiply_convert_fusion), channel_id=1, source_target_pairs={{0,3},{1,0},{2,1},{3,2},{4,7},{5,4},{6,5},{7,6},{8,11},{9,8},{10,9... | collective-permute-start | bytes 27656 | tf_op jit(solution)/shard_map/ppermute | solution.py:42
  14.6 2.5 collective-permute-start.8
  20.0 1.7 dynamic-slice_bitcast_fusion.1
  26.7 2.9 collective-permute-start.6
  34.6 3.3 collective-permute-done.16
  42.6 2.1 collective-permute-done.17
  51.9 7.4 %collective-permute-done.9.refs_3_ = bf16[96,1152]{1,0:T(8,128)(2,1)S(1)} collective-permute-done((bf16[96,1152]{1,0:T(8,128)(2,1)}, bf16[96,1152]{1,0:T(8,128)(2,1)S(1)}, u32[]{:S(2)}, u32[]{:S(2)}) %collective-permute-start.9) | collective-permute-done | bytes 221216 | tf_op jit(solution)/shard_map/ppermute | solution.py:42
  59.4 10.5 %collective-permute-done.10.refs_4_.refs_2_ = bf16[96,1152]{1,0:T(8,128)(2,1)S(1)} collective-permute-done((bf16[96,1152]{1,0:T(8,128)(2,1)S(1)}, bf16[96,1152]{1,0:T(8,128)(2,1)S(1)}, u32[]{:S(2)}, u32[]{:S(2)}) %collective-permute-start.10) | collective-permute-done | bytes 221216 | tf_op jit(solution)/shard_map/ppermute | solution.py:42
  75.5 2.7 collective-permute-done.12.refs_6_
  78.2 4.7 %collective-permute-done.13.refs_7_ = bf16[96,1152]{1,0:T(8,128)(2,1)S(1)} collective-permute-done((bf16[96,1152]{1,0:T(8,128)(2,1)S(1)}, bf16[96,1152]{1,0:T(8,128)(2,1)S(1)}, u32[]{:S(2)}, u32[]{:S(2)}) %collective-permute-start.13) | collective-permute-done | bytes 221216 | tf_op jit(solution)/shard_map/ppermute | solution.py:37
  84.5 2.3 shard_map.145.w_ref.wqkv_ref
  88.0 7.2 %shard_map.146 = (bf16[3,256,1152]{2,1,0:T(8,128)(2,1)}, bf16[3,256,384]{2,1,0:T(8,128)(2,1)S(1)}) custom-call(bf16[3,256,768]{2,1,0:T(8,128)(2,1)S(1)} %pad_maximum_fusion.h_ref.g_ref, f32[3,6,768]{2,1,0:T(8,128)S(1)} %copy-done.16, bf16[768,1152]{1,0:T(8,128)(2,1)S(1)} %shard_map.145.w_ref.wqkv_ref), custom_call_target="tpu_custom_call" | custom-call | flops 3170893824 | bytes 8388608 | tf_op jit(solution)/shard_map/pallas_call | solution.py:294
  98.4 8.0 %collective-permute-done.24.refs_4_ = bf16[96,1536]{1,0:T(8,128)(2,1)S(1)} collective-permute-done((bf16[96,1536]{1,0:T(8,128)(2,1)S(1)}, bf16[96,1536]{1,0:T(8,128)(2,1)S(1)}, u32[]{:S(2)}, u32[]{:S(2)}) %collective-permute-start.24) | collective-permute-done | bytes 294944 | tf_op jit(solution)/shard_map/ppermute | solution.py:42
  110.3 1.8 collective-permute-done.25.refs_5_
  112.0 6.3 %collective-permute-done.26.refs_6_ = bf16[96,1536]{1,0:T(8,128)(2,1)S(1)} collective-permute-done((bf16[96,1536]{1,0:T(8,128)(2,1)S(1)}, bf16[96,1536]{1,0:T(8,128)(2,1)S(1)}, u32[]{:S(2)}, u32[]{:S(2)}) %collective-permute-start.26) | collective-permute-done | bytes 294944 | tf_op jit(solution)/shard_map/ppermute | solution.py:37
  118.4 5.6 %collective-permute-done.27.refs_7_ = bf16[96,1536]{1,0:T(8,128)(2,1)S(1)} collective-permute-done((bf16[96,1536]{1,0:T(8,128)(2,1)S(1)}, bf16[96,1536]{1,0:T(8,128)(2,1)S(1)}, u32[]{:S(2)}, u32[]{:S(2)}) %collective-permute-start.27) | collective-permute-done | bytes 294944 | tf_op jit(solution)/shard_map/ppermute | solution.py:37
  126.6 10.9 %shard_map.150 = (bf16[3,256,768]{2,1,0:T(8,128)(2,1)}, f32[3,256,768]{2,1,0:T(8,128)}) custom-call(s32[3]{0:T(128)S(1)} %pad_add_fusion.refs_0_.place, bf16[3,256,768]{2,1,0:T(8,128)(2,1)S(1)} %pad_maximum_fusion.h_ref.g_ref, f32[3,6,768]{2,1,0:T(8,128)S(1)} %copy-done.16, bf16[3,256,384]{2,1,0:T(8,128)(2,1)S(1)} %get-tuple-element.38.own_ref, ...), custom_call_target="tpu_custom_call" | custom-call | flops 4529848320 | bytes 16777216 | tf_op jit(solution)/shard_map/pallas_call | solution.py:340
  138.4 2.1 collective-permute-done.34
  141.6 1.8 fusion.8
  143.4 3.9 collective-permute-start.35
  147.3 12.4 %collective-permute-done.35 = bf16[3,128,768]{2,1,0:T(8,128)(2,1)S(1)} collective-permute-done((bf16[3,128,768]{2,1,0:T(8,128)(2,1)S(1)}, bf16[3,128,768]{2,1,0:T(8,128)(2,1)S(1)}, u32[]{:S(2)}, u32[]{:S(2)}) %collective-permute-start.35) | collective-permute-done | bytes 589856 | tf_op jit(solution)/shard_map/ppermute | solution.py:516
  159.7 2.0 collective-permute-done.36
  162.7 8.3 %shard_map.151 = (bf16[3,256,1152]{2,1,0:T(8,128)(2,1)S(1)}, bf16[3,256,384]{2,1,0:T(8,128)(2,1)S(1)}, bf16[3,256,768]{2,1,0:T(8,128)(2,1)S(1)}) custom-call(bf16[3,256,768]{2,1,0:T(8,128)(2,1)S(1)} %maximum_select_fusion.h_ref, f32[3,6,768]{2,1,0:T(8,128)S(1)} %copy-done.17, bf16[768,1152]{1,0:T(8,128)(2,1)} %copy-done.6), custom_call_target="tpu_custom_call" | custom-call | flops 3170893824 | bytes 8388608 | tf_op jit(solution)/shard_map/pallas_call | solution.py:294
  173.4 1.9 collective-permute-done.37.other_ref
  175.3 12.3 %shard_map.152 = (bf16[3,256,768]{2,1,0:T(8,128)(2,1)S(1)}, f32[3,256,768]{2,1,0:T(8,128)}, bf16[3,256,768]{2,1,0:T(8,128)(2,1)S(1)}, bf16[3,256,768]{2,1,0:T(8,...) custom-call(s32[3]{0:T(128)S(1)} %pad_add_fusion.refs_0_.place, ...), custom_call_target="tpu_custom_call" | custom-call | flops 4529848320 | bytes 16777216 | tf_op jit(solution)/shard_map/pallas_call | solution.py:340
  190.8 9.2 %shard_map.153 = (bf16[3,256,768]{2,1,0:T(8,128)(2,1)S(1)}, bf16[3,256,1536]{2,1,0:T(8,128)(2,1)}) custom-call(bf16[3,256,768]{2,1,0:T(8,128)(2,1)S(1)} %copy-done.11, f32[3,6,768]{2,1,0:T(8,128)S(1)} %copy-done.17, f32[3,256,1536]{2,1,0:T(8,128)} %get-tuple-element.44.pre_ref, bf16[1536,768]{1,0:T(8,128)(2,1)} %copy-done.4, bf16[768,1536]{1,0:T(8,128)(2,1)} %copy-done.5), custom_call_target="tpu_custom_call" | custom-call | flops 3623878656 | bytes 14680064 | tf_op jit(solution)/shard_map/pallas_call | solution.py:367
  200.1 2.7 collective-permute-done.38.other_ref
  202.8 15.0 %shard_map.154 = (bf16[3,256,768]{2,1,0:T(8,128)(2,1)S(1)}, f32[3,256,768]{2,1,0:T(8,128)}, bf16[3,256,768]{2,1,0:T(8,128)(2,1)}, bf16[3,256,1152]{2,1,0:T(8,128)(2,1)}, f32[3,3,768]{2,1,0:T(4,128)}) custom-call(s32[3]{0:T(128)S(1)} %pad_add_fusion.refs_0_.place, bf16[3,256,768]{2,1,0:T(8,128)(2,1)S(1)} %get-tuple-element.45.own_ref, ...), custom_call_target="tpu_custom_call" | custom-call | flops 5888802816 | bytes 14680064 | tf_op jit(solution)/shard_map/pallas_call | solution.py:419
  217.9 2.7 collective-permute-done.39.other_ref
  220.6 4.2 shard_map.155
  226.3 16.0 %collective-permute-done.40 = bf16[3,128,768]{2,1,0:T(8,128)(2,1)} collective-permute-done((bf16[3,128,768]{2,1,0:T(8,128)(2,1)S(1)}, bf16[3,128,768]{2,1,0:T(8,128)(2,1)}, u32[]{:S(2)}, u32[]{:S(2)}) %collective-permute-start.40) | collective-permute-done | bytes 589856 | tf_op jit(solution)/shard_map/ppermute | solution.py:516
  242.3 4.3 copy.80
  246.6 2.4 copy.76
  252.7 2.0 fusion.49
  257.3 8.7 %shard_map.156 = (bf16[3,256,768]{2,1,0:T(8,128)(2,1)S(1)}, bf16[3,256,1536]{2,1,0:T(8,128)(2,1)S(1)}) custom-call(bf16[3,256,768]{2,1,0:T(8,128)(2,1)S(1)} %get-tuple-element.101.g_ref, f32[3,6,768]{2,1,0:T(8,128)S(1)} %copy-done.17, f32[3,256,1536]{2,1,0:T(8,128)} %get-tuple-element.44.pre_ref, bf16[1536,768]{1,0:T(8,128)(2,1)} %copy-done.4, ...), custom_call_target="tpu_custom_call" | custom-call | flops 3623878656 | bytes 14680064 | tf_op jit(solution)/shard_map/pallas_call | solution.py:367
  266.0 2.0 fusion.48
  271.2 2.4 copy.71
  275.5 9.5 %collective-permute-done.69 = bf16[4,192,768]{2,1,0:T(8,128)(2,1)} collective-permute-done((bf16[4,192,768]{2,1,0:T(8,128)(2,1)}, bf16[4,192,768]{2,1,0:T(8,128)(2,1)}, u32[]{:S(2)}, u32[]{:S(2)}) %collective-permute-start.69) | collective-permute-done | bytes 1179680 | tf_op jit(solution)/shard_map/ppermute | solution.py:37
  285.0 2.4 bitcast_add_fusion
  288.3 21.6 %collective-permute-done.63 = bf16[4,96,1536]{2,1,0:T(8,128)(2,1)} collective-permute-done((bf16[4,96,1536]{2,1,0:T(8,128)(2,1)}, bf16[4,96,1536]{2,1,0:T(8,128)(2,1)}, u32[]{:S(2)}, u32[]{:S(2)}) %collective-permute-start.63) | collective-permute-done | bytes 1179680 | tf_op jit(solution)/shard_map/ppermute | solution.py:37
  311.8 15.9 %shard_map.157 = (bf16[3,256,768]{2,1,0:T(8,128)(2,1)}, f32[3,256,768]{2,1,0:T(8,128)}, bf16[3,256,768]{2,1,0:T(8,128)(2,1)S(1)}, bf16[3,256,1152]{2,1,0:T(8,128)(2,1)}, f32[3,3,768]{2,1,0:T(4,128)S(1)}) custom-call(s32[3]{0:T(128)S(1)} %pad_add_fusion.refs_0_.place, bf16[3,256,768]{2,1,0:T(8,128)(2,1)S(1)} %copy-done.23, ...), custom_call_target="tpu_custom_call" | custom-call | flops 5888802816 | bytes 14680064 | tf_op jit(solution)/shard_map/pallas_call | solution.py:419
  328.5 3.2 collective-permute-start.58
  331.7 1.7 fusion.47
  338.6 11.2 %collective-permute-done.59 = bf16[192,384]{1,0:T(8,128)(2,1)S(1)} collective-permute-done((bf16[192,384]{1,0:T(8,128)(2,1)S(1)}, bf16[192,384]{1,0:T(8,128)(2,1)S(1)}, u32[]{:S(2)}, u32[]{:S(2)}) %collective-permute-start.59) | collective-permute-done | bytes 147488 | tf_op jit(solution)/shard_map/ppermute | solution.py:42
  351.7 10.2 %collective-permute-done.60 = bf16[192,384]{1,0:T(8,128)(2,1)S(1)} collective-permute-done((bf16[192,384]{1,0:T(8,128)(2,1)S(1)}, bf16[192,384]{1,0:T(8,128)(2,1)S(1)}, u32[]{:S(2)}, u32[]{:S(2)}) %collective-permute-start.60) | collective-permute-done | bytes 147488 | tf_op jit(solution)/shard_map/ppermute | solution.py:42
  363.5 3.7 collective-permute-done.61
  367.2 6.4 %collective-permute-done.65 = bf16[96,1536]{1,0:T(8,128)(2,1)S(1)} collective-permute-done((bf16[96,1536]{1,0:T(8,128)(2,1)S(1)}, bf16[96,1536]{1,0:T(8,128)(2,1)S(1)}, u32[]{:S(2)}, u32[]{:S(2)}) %collective-permute-start.65) | collective-permute-done | bytes 294944 | tf_op jit(solution)/shard_map/ppermute | solution.py:42
  376.4 2.3 reshape.556
  378.7 10.3 %collective-permute-done.72 = bf16[192,768]{1,0:T(8,128)(2,1)} collective-permute-done((bf16[192,768]{1,0:T(8,128)(2,1)}, bf16[192,768]{1,0:T(8,128)(2,1)}, u32[]{:S(2)}, u32[]{:S(2)}) %collective-permute-start.72) | collective-permute-done | bytes 294944 | tf_op jit(solution)/shard_map/ppermute | solution.py:42
  394.0 2.1 fusion.14
  396.1 2.7 collective-permute-done.73
  399.8 2.1 collective-permute-done.67
  402.9 4.4 shard_map.158
  407.3 2.0 fusion
  414.3 3.6 collective-permute-done.47
  417.9 5.6 %collective-permute-done.48 = bf16[6,4608]{1,0:T(8,128)(2,1)S(1)} collective-permute-done((bf16[6,4608]{1,0:T(8,128)(2,1)S(1)}, bf16[6,4608]{1,0:T(8,128)(2,1)S(1)}, u32[]{:S(2)}, u32[]{:S(2)}) %collective-permute-start.48) | collective-permute-done | bytes 55328 | tf_op jit(solution)/shard_map/ppermute | solution.py:42
  423.5 6.2 %collective-permute-done.49 = bf16[6,4608]{1,0:T(8,128)(2,1)S(1)} collective-permute-done((bf16[6,4608]{1,0:T(8,128)(2,1)S(1)}, bf16[6,4608]{1,0:T(8,128)(2,1)S(1)}, u32[]{:S(2)}, u32[]{:S(2)}) %collective-permute-start.49) | collective-permute-done | bytes 55328 | tf_op jit(solution)/shard_map/ppermute | solution.py:42
  434.3 4.5 collective-permute-done.51
  439.3 5.2 %collective-permute-done.52 = f32[6,192]{1,0:T(8,128)S(1)} collective-permute-done((f32[6,192]{1,0:T(8,128)S(1)}, f32[6,192]{1,0:T(8,128)S(1)}, u32[]{:S(2)}, u32[]{:S(2)}) %collective-permute-start.52) | collective-permute-done | bytes 4640 | tf_op jit(solution)/shard_map/ppermute | solution.py:42
  445.4 2.1 fusion.15
  452.0 3.2 copy.79
  455.3 4.1 reshape.557
  465.6 2.6 reshape.555
  (357 shorter events, 113.9 us)
Async XLA Ops:
  5.2 16.6 %collective-permute-start.2 = (bf16[6,768]{1,0:T(8,128)(2,1)S(1)}, bf16[6,768]{1,0:T(8,128)(2,1)S(1)}, u32[]{:S(2)}, u32[]{:S(2)}) collective-permute-start(bf16[6,768]{1,0:T(8,128)(2,1)S(1)} %multiply_convert_fusion), channel_id=1, source_target_pairs={{0,3},{1,0},{2,1},{3,2},{4,7},{5,4},{6,5},{7,6},{8,11},{9,8},{10,9... | collective-permute-start | bytes 27656 | tf_op jit(solution)/shard_map/ppermute | solution.py:42
  10.3 11.5 %collective-permute-start.3 = (bf16[6,768]{1,0:T(8,128)(2,1)S(1)}, bf16[6,768]{1,0:T(8,128)(2,1)S(1)}, u32[]{:S(2)}, u32[]{:S(2)}) collective-permute-start(bf16[6,768]{1,0:T(8,128)(2,1)S(1)} %multiply_convert_fusion), channel_id=1, source_target_pairs={{0,2},{1,3},{2,0},{3,1},{4,6},{5,7},{6,4},{7,5},{8,10},{9,11},{10,... | collective-permute-start | bytes 27656 | tf_op jit(solution)/shard_map/ppermute | solution.py:42
  10.3 11.5 %collective-permute-start.4 = (bf16[6,768]{1,0:T(8,128)(2,1)S(1)}, bf16[6,768]{1,0:T(8,128)(2,1)S(1)}, u32[]{:S(2)}, u32[]{:S(2)}) collective-permute-start(bf16[6,768]{1,0:T(8,128)(2,1)S(1)} %multiply_convert_fusion), channel_id=1, source_target_pairs={{0,1},{1,2},{2,3},{3,0},{4,5},{5,6},{6,7},{7,4},{8,9},{9,10},{10,1... | collective-permute-start | bytes 27656 | tf_op jit(solution)/shard_map/ppermute | solution.py:42
  14.6 34.3 %collective-permute-start.8 = (bf16[96,1152]{1,0:T(8,128)(2,1)}, bf16[96,1152]{1,0:T(8,128)(2,1)}, u32[]{:S(2)}, u32[]{:S(2)}) collective-permute-start(bf16[96,1152]{1,0:T(8,128)(2,1)} %get-tuple-element.37), channel_id=1, source_target_pairs={{0,1},{1,2},{2,3},{3,0},{4,5},{5,6},{6,7},{7,4},{8,9},{9,10},{10,1... | collective-permute-start | bytes 663560 | tf_op jit(solution)/shard_map/ppermute | solution.py:42
  18.0 12.8 %collective-permute-start.15 = (bf16[48,768]{1,0:T(8,128)(2,1)S(1)}, bf16[48,768]{1,0:T(8,128)(2,1)}, u32[]{:S(2)}, u32[]{:S(2)}) collective-permute-start(bf16[48,768]{1,0:T(8,128)(2,1)S(1)} %dynamic-slice_bitcast_fusion.4), channel_id=1, source_target_pairs={{0,1},{1,2},{2,3},{3,0},{4,5},{5,6},{6,7},{7,4},{8,9},{9,10},{10,1... | collective-permute-start | bytes 221192 | tf_op jit(solution)/shard_map/ppermute | solution.py:42
  24.6 7.9 %collective-permute-start.5 = (f32[3,4608]{1,0:T(4,128)}, f32[3,4608]{1,0:T(4,128)}, u32[]{:S(2)}, u32[]{:S(2)}) collective-permute-start(f32[3,4608]{1,0:T(4,128)} %bitcast.239), channel_id=1, source_target_pairs={{0,1},{1,2},{2,3},{3,0},{4,5},{5,6},{6,7},{7,4},{8,9},{9,10},{10,1... | collective-permute-start | bytes 165896 | tf_op jit(solution)/shard_map/ppermute | solution.py:42
  26.7 7.9 %collective-permute-start.6 = (f32[3,4608]{1,0:T(4,128)}, f32[3,4608]{1,0:T(4,128)}, u32[]{:S(2)}, u32[]{:S(2)}) collective-permute-start(f32[3,4608]{1,0:T(4,128)} %bitcast.238), channel_id=1, source_target_pairs={{0,2},{1,3},{2,0},{3,1},{4,6},{5,7},{6,4},{7,5},{8,10},{9,11},{10,... | collective-permute-start | bytes 165896 | tf_op jit(solution)/shard_map/ppermute | solution.py:42
  30.3 7.6 %collective-permute-start.7 = (f32[3,4608]{1,0:T(4,128)}, f32[3,4608]{1,0:T(4,128)}, u32[]{:S(2)}, u32[]{:S(2)}) collective-permute-start(f32[3,4608]{1,0:T(4,128)} %bitcast.237), channel_id=1, source_target_pairs={{0,3},{1,0},{2,1},{3,2},{4,7},{5,4},{6,5},{7,6},{8,11},{9,8},{10,9... | collective-permute-start | bytes 165896 | tf_op jit(solution)/shard_map/ppermute | solution.py:42
  30.7 7.2 %collective-permute-start.16 = (bf16[48,768]{1,0:T(8,128)(2,1)}, bf16[48,768]{1,0:T(8,128)(2,1)}, u32[]{:S(2)}, u32[]{:S(2)}) collective-permute-start(bf16[48,768]{1,0:T(8,128)(2,1)} %collective-permute-done.15), channel_id=1, source_target_pairs={{0,1},{1,2},{2,3},{3,0},{4,5},{5,6},{6,7},{7,4},{8,9},{9,10},{10,1... | collective-permute-start | bytes 221192 | tf_op jit(solution)/shard_map/ppermute | solution.py:42
  32.4 13.8 %collective-permute-start = (bf16[3,64,768]{2,1,0:T(8,128)(2,1)}, bf16[3,64,768]{2,1,0:T(8,128)(2,1)}, u32[]{:S(2)}, u32[]{:S(2)}) collective-permute-start(bf16[3,64,768]{2,1,0:T(8,128)(2,1)} %get-tuple-element.124), channel_id=1, source_target_pairs={{0,8},{4,12},{8,0},{12,4},{1,9},{5,13},{9,1},{13,5},{2,10},{6,14},... | collective-permute-start | bytes 884744 | tf_op jit(solution)/shard_map/ppermute | solution.py:37
  34.6 16.2 %collective-permute-start.28 = (bf16[192,768]{1,0:T(8,128)(2,1)}, bf16[192,768]{1,0:T(8,128)(2,1)}, u32[]{:S(2)}, u32[]{:S(2)}) collective-permute-start(bf16[192,768]{1,0:T(8,128)(2,1)} %dynamic-slice_bitcast_fusion.1), channel_id=1, source_target_pairs={{0,1},{1,2},{2,3},{3,0},{4,5},{5,6},{6,7},{7,4},{8,9},{9,10},{10,1... | collective-permute-start | bytes 884744 | tf_op jit(solution)/shard_map/ppermute | solution.py:42
  37.9 6.8 %collective-permute-start.17 = (bf16[48,768]{1,0:T(8,128)(2,1)}, bf16[48,768]{1,0:T(8,128)(2,1)}, u32[]{:S(2)}, u32[]{:S(2)}) collective-permute-start(bf16[48,768]{1,0:T(8,128)(2,1)} %collective-permute-done.16), channel_id=1, source_target_pairs={{0,1},{1,2},{2,3},{3,0},{4,5},{5,6},{6,7},{7,4},{8,9},{9,10},{10,1... | collective-permute-start | bytes 221192 | tf_op jit(solution)/shard_map/ppermute | solution.py:42
  41.1 6.8 %collective-permute-start.18 = (bf16[48,768]{1,0:T(8,128)(2,1)}, bf16[48,768]{1,0:T(8,128)(2,1)S(1)}, u32[]{:S(2)}, u32[]{:S(2)}) collective-permute-start(bf16[48,768]{1,0:T(8,128)(2,1)} %collective-permute-done.15), channel_id=1, source_target_pairs={{0,8},{4,12},{8,0},{12,4},{1,9},{5,13},{9,1},{13,5},{2,10},{6,14},... | collective-permute-start | bytes 221192 | tf_op jit(solution)/shard_map/ppermute | solution.py:37
  44.7 4.6 collective-permute-start.19
  46.2 5.5 %collective-permute-start.20 = (bf16[48,768]{1,0:T(8,128)(2,1)}, bf16[48,768]{1,0:T(8,128)(2,1)S(1)}, u32[]{:S(2)}, u32[]{:S(2)}) collective-permute-start(bf16[48,768]{1,0:T(8,128)(2,1)} %collective-permute-done.17), channel_id=1, source_target_pairs={{0,8},{4,12},{8,0},{12,4},{1,9},{5,13},{9,1},{13,5},{2,10},{6,14},... | collective-permute-start | bytes 221192 | tf_op jit(solution)/shard_map/ppermute | solution.py:37
  47.9 24.3 %collective-permute-start.1 = (bf16[3,128,768]{2,1,0:T(8,128)(2,1)S(1)}, bf16[3,128,768]{2,1,0:T(8,128)(2,1)S(1)}, u32[]{:S(2)}, u32[]{:S(2)}) collective-permute-start(bf16[3,128,768]{2,1,0:T(8,128)(2,1)S(1)} %pad_maximum_fusion.1), channel_id=1, source_target_pairs={{0,4},{4,0},{8,12},{12,8},{1,5},{5,1},{9,13},{13,9},{2,6},{6,2},{1... | collective-permute-start | bytes 1769480 | tf_op jit(solution)/shard_map/ppermute | solution.py:33
  48.9 10.3 %collective-permute-start.9 = (bf16[96,1152]{1,0:T(8,128)(2,1)}, bf16[96,1152]{1,0:T(8,128)(2,1)S(1)}, u32[]{:S(2)}, u32[]{:S(2)}) collective-permute-start(bf16[96,1152]{1,0:T(8,128)(2,1)} %collective-permute-done.8.refs_2_), channel_id=1, source_target_pairs={{0,1},{1,2},{2,3},{3,0},{4,5},{5,6},{6,7},{7,4},{8,9},{9,10},{10,1... | collective-permute-start | bytes 663560 | tf_op jit(solution)/shard_map/ppermute | solution.py:42
  49.3 22.7 %collective-permute-start.11 = (bf16[96,1152]{1,0:T(8,128)(2,1)}, bf16[96,1152]{1,0:T(8,128)(2,1)S(1)}, u32[]{:S(2)}, u32[]{:S(2)}) collective-permute-start(bf16[96,1152]{1,0:T(8,128)(2,1)} %collective-permute-done.8.refs_2_), channel_id=1, source_target_pairs={{0,8},{4,12},{8,0},{12,4},{1,9},{5,13},{9,1},{13,5},{2,10},{6,14},... | collective-permute-start | bytes 663560 | tf_op jit(solution)/shard_map/ppermute | solution.py:37
  50.8 23.1 %collective-permute-start.29 = (bf16[192,768]{1,0:T(8,128)(2,1)}, bf16[192,768]{1,0:T(8,128)(2,1)S(1)}, u32[]{:S(2)}, u32[]{:S(2)}) collective-permute-start(bf16[192,768]{1,0:T(8,128)(2,1)} %collective-permute-done.28.refs_2_), channel_id=1, source_target_pairs={{0,1},{1,2},{2,3},{3,0},{4,5},{5,6},{6,7},{7,4},{8,9},{9,10},{10,1... | collective-permute-start | bytes 884744 | tf_op jit(solution)/shard_map/ppermute | solution.py:42
  59.2 10.7 %collective-permute-start.10 = (bf16[96,1152]{1,0:T(8,128)(2,1)S(1)}, bf16[96,1152]{1,0:T(8,128)(2,1)S(1)}, u32[]{:S(2)}, u32[]{:S(2)}) collective-permute-start(bf16[96,1152]{1,0:T(8,128)(2,1)S(1)} %collective-permute-done.9.refs_3_), channel_id=1, source_target_pairs={{0,1},{1,2},{2,3},{3,0},{4,5},{5,6},{6,7},{7,4},{8,9},{9,10},{10,1... | collective-permute-start | bytes 663560 | tf_op jit(solution)/shard_map/ppermute | solution.py:42
  59.3 35.9 %collective-permute-start.21 = (bf16[3,2,48,768]{3,2,1,0:T(8,128)(2,1)S(1)}, bf16[3,2,48,768]{3,2,1,0:T(8,128)(2,1)S(1)}, u32[]{:S(2)}, u32[]{:S(2)}) collective-permute-start(bf16[3,2,48,768]{3,2,1,0:T(8,128)(2,1)S(1)} %reverse_select_fusion), channel_id=1, source_target_pairs={{0,4},{4,0},{8,12},{12,8},{1,5},{5,1},{9,13},{13,9},{2,6},{6,2},{1... | collective-permute-start | bytes 1327112 | tf_op jit(solution)/shard_map/ppermute | solution.py:33
  69.9 8.3 %collective-permute-start.12 = (bf16[96,1152]{1,0:T(8,128)(2,1)S(1)}, bf16[96,1152]{1,0:T(8,128)(2,1)S(1)}, u32[]{:S(2)}, u32[]{:S(2)}) collective-permute-start(bf16[96,1152]{1,0:T(8,128)(2,1)S(1)} %collective-permute-done.9.refs_3_), channel_id=1, source_target_pairs={{0,8},{4,12},{8,0},{12,4},{1,9},{5,13},{9,1},{13,5},{2,10},{6,14},... | collective-permute-start | bytes 663560 | tf_op jit(solution)/shard_map/ppermute | solution.py:37
  72.0 14.9 %collective-permute-start.22 = (bf16[96,1536]{1,0:T(8,128)(2,1)S(1)}, bf16[96,1536]{1,0:T(8,128)(2,1)S(1)}, u32[]{:S(2)}, u32[]{:S(2)}) collective-permute-start(bf16[96,1536]{1,0:T(8,128)(2,1)S(1)} %get-tuple-element.40), channel_id=1, source_target_pairs={{0,1},{1,2},{2,3},{3,0},{4,5},{5,6},{6,7},{7,4},{8,9},{9,10},{10,1... | collective-permute-start | bytes 884744 | tf_op jit(solution)/shard_map/ppermute | solution.py:42
  72.1 10.8 %collective-permute-start.13 = (bf16[96,1152]{1,0:T(8,128)(2,1)S(1)}, bf16[96,1152]{1,0:T(8,128)(2,1)S(1)}, u32[]{:S(2)}, u32[]{:S(2)}) collective-permute-start(bf16[96,1152]{1,0:T(8,128)(2,1)S(1)} %collective-permute-done.10.refs_4_.refs_2_), channel_id=1, source_target_pairs={{0,8},{4,12},{8,0},{12,4},{1,9},{5,13},{9,1},{13,5},{2,10},{6,14},... | collective-permute-start | bytes 663560 | tf_op jit(solution)/shard_map/ppermute | solution.py:37
  73.9 22.5 %collective-permute-start.31 = (bf16[192,768]{1,0:T(8,128)(2,1)}, bf16[192,768]{1,0:T(8,128)(2,1)S(1)}, u32[]{:S(2)}, u32[]{:S(2)}) collective-permute-start(bf16[192,768]{1,0:T(8,128)(2,1)} %collective-permute-done.28.refs_2_), channel_id=1, source_target_pairs={{0,8},{4,12},{8,0},{12,4},{1,9},{5,13},{9,1},{13,5},{2,10},{6,14},... | collective-permute-start | bytes 884744 | tf_op jit(solution)/shard_map/ppermute | solution.py:37
  78.2 17.6 %collective-permute-start.30 = (bf16[192,768]{1,0:T(8,128)(2,1)S(1)}, bf16[192,768]{1,0:T(8,128)(2,1)S(1)}, u32[]{:S(2)}, u32[]{:S(2)}) collective-permute-start(bf16[192,768]{1,0:T(8,128)(2,1)S(1)} %collective-permute-done.29.refs_3_), channel_id=1, source_target_pairs={{0,1},{1,2},{2,3},{3,0},{4,5},{5,6},{6,7},{7,4},{8,9},{9,10},{10,1... | collective-permute-start | bytes 884744 | tf_op jit(solution)/shard_map/ppermute | solution.py:42
  83.0 15.0 %collective-permute-start.32 = (bf16[192,768]{1,0:T(8,128)(2,1)S(1)}, bf16[192,768]{1,0:T(8,128)(2,1)S(1)}, u32[]{:S(2)}, u32[]{:S(2)}) collective-permute-start(bf16[192,768]{1,0:T(8,128)(2,1)S(1)} %collective-permute-done.29.refs_3_), channel_id=1, source_target_pairs={{0,8},{4,12},{8,0},{12,4},{1,9},{5,13},{9,1},{13,5},{2,10},{6,14},... | collective-permute-start | bytes 884744 | tf_op jit(solution)/shard_map/ppermute | solution.py:37
  86.9 8.6 %collective-permute-start.23 = (bf16[96,1536]{1,0:T(8,128)(2,1)S(1)}, bf16[96,1536]{1,0:T(8,128)(2,1)S(1)}, u32[]{:S(2)}, u32[]{:S(2)}) collective-permute-start(bf16[96,1536]{1,0:T(8,128)(2,1)S(1)} %collective-permute-done.22.refs_2_), channel_id=1, source_target_pairs={{0,1},{1,2},{2,3},{3,0},{4,5},{5,6},{6,7},{7,4},{8,9},{9,10},{10,1... | collective-permute-start | bytes 884744 | tf_op jit(solution)/shard_map/ppermute | solution.py:42
  95.2 31.3 %collective-permute-start.14 = (bf16[3,256,384]{2,1,0:T(8,128)(2,1)S(1)}, bf16[3,256,384]{2,1,0:T(8,128)(2,1)S(1)}, u32[]{:S(2)}, u32[]{:S(2)}) collective-permute-start(bf16[3,256,384]{2,1,0:T(8,128)(2,1)S(1)} %get-tuple-element.38.own_ref), channel_id=1, source_target_pairs={{0,4},{4,0},{8,12},{12,8},{1,5},{5,1},{9,13},{13,9},{2,6},{6,2},{1... | collective-permute-start | bytes 1769480 | tf_op jit(solution)/shard_map/ppermute | solution.py:33
  95.5 11.0 %collective-permute-start.24 = (bf16[96,1536]{1,0:T(8,128)(2,1)S(1)}, bf16[96,1536]{1,0:T(8,128)(2,1)S(1)}, u32[]{:S(2)}, u32[]{:S(2)}) collective-permute-start(bf16[96,1536]{1,0:T(8,128)(2,1)S(1)} %collective-permute-done.23.refs_3_), channel_id=1, source_target_pairs={{0,1},{1,2},{2,3},{3,0},{4,5},{5,6},{6,7},{7,4},{8,9},{9,10},{10,1... | collective-permute-start | bytes 884744 | tf_op jit(solution)/shard_map/ppermute | solution.py:42
  95.8 11.3 %collective-permute-start.33 = (bf16[192,768]{1,0:T(8,128)(2,1)S(1)}, bf16[192,768]{1,0:T(8,128)(2,1)S(1)}, u32[]{:S(2)}, u32[]{:S(2)}) collective-permute-start(bf16[192,768]{1,0:T(8,128)(2,1)S(1)} %collective-permute-done.30.refs_4_), channel_id=1, source_target_pairs={{0,8},{4,12},{8,0},{12,4},{1,9},{5,13},{9,1},{13,5},{2,10},{6,14},... | collective-permute-start | bytes 884744 | tf_op jit(solution)/shard_map/ppermute | solution.py:37
  96.4 15.6 %collective-permute-start.25 = (bf16[96,1536]{1,0:T(8,128)(2,1)S(1)}, bf16[96,1536]{1,0:T(8,128)(2,1)S(1)}, u32[]{:S(2)}, u32[]{:S(2)}) collective-permute-start(bf16[96,1536]{1,0:T(8,128)(2,1)S(1)} %collective-permute-done.22.refs_2_), channel_id=1, source_target_pairs={{0,8},{4,12},{8,0},{12,4},{1,9},{5,13},{9,1},{13,5},{2,10},{6,14},... | collective-permute-start | bytes 884744 | tf_op jit(solution)/shard_map/ppermute | solution.py:37
  97.9 20.4 %collective-permute-start.26 = (bf16[96,1536]{1,0:T(8,128)(2,1)S(1)}, bf16[96,1536]{1,0:T(8,128)(2,1)S(1)}, u32[]{:S(2)}, u32[]{:S(2)}) collective-permute-start(bf16[96,1536]{1,0:T(8,128)(2,1)S(1)} %collective-permute-done.23.refs_3_), channel_id=1, source_target_pairs={{0,8},{4,12},{8,0},{12,4},{1,9},{5,13},{9,1},{13,5},{2,10},{6,14},... | collective-permute-start | bytes 884744 | tf_op jit(solution)/shard_map/ppermute | solution.py:37
  106.5 17.5 %collective-permute-start.27 = (bf16[96,1536]{1,0:T(8,128)(2,1)S(1)}, bf16[96,1536]{1,0:T(8,128)(2,1)S(1)}, u32[]{:S(2)}, u32[]{:S(2)}) collective-permute-start(bf16[96,1536]{1,0:T(8,128)(2,1)S(1)} %collective-permute-done.24.refs_4_), channel_id=1, source_target_pairs={{0,8},{4,12},{8,0},{12,4},{1,9},{5,13},{9,1},{13,5},{2,10},{6,14},... | collective-permute-start | bytes 884744 | tf_op jit(solution)/shard_map/ppermute | solution.py:37
  143.4 16.3 %collective-permute-start.35 = (bf16[3,128,768]{2,1,0:T(8,128)(2,1)S(1)}, bf16[3,128,768]{2,1,0:T(8,128)(2,1)S(1)}, u32[]{:S(2)}, u32[]{:S(2)}) collective-permute-start(bf16[3,128,768]{2,1,0:T(8,128)(2,1)S(1)} %fusion.8), channel_id=1, source_target_pairs={{0,16},{1,17},{2,18},{3,19},{4,20},{5,21},{6,22},{7,23},{8,24},{9,... | collective-permute-start | bytes 1769480 | tf_op jit(solution)/shard_map/ppermute | solution.py:516
  224.8 17.5 %collective-permute-start.40 = (bf16[3,128,768]{2,1,0:T(8,128)(2,1)S(1)}, bf16[3,128,768]{2,1,0:T(8,128)(2,1)}, u32[]{:S(2)}, u32[]{:S(2)}) collective-permute-start(bf16[3,128,768]{2,1,0:T(8,128)(2,1)S(1)} %constant_dynamic-slice_fusion.6), channel_id=1, source_target_pairs={{16,0},{17,1},{18,2},{19,3},{20,4},{21,5},{22,6},{23,7},{24,8},{25... | collective-permute-start | bytes 1769480 | tf_op jit(solution)/shard_map/ppermute | solution.py:516
  242.3 6.7 %collective-permute-start.41 = (bf16[3,128,768]{2,1,0:T(8,128)(2,1)}, bf16[3,128,768]{2,1,0:T(8,128)(2,1)}, u32[]{:S(2)}, u32[]{:S(2)}) collective-permute-start(bf16[3,128,768]{2,1,0:T(8,128)(2,1)} %collective-permute-done.40), channel_id=1, source_target_pairs={{0,4},{4,0},{8,12},{12,8},{1,5},{5,1},{9,13},{13,9},{2,6},{6,2},{1... | collective-permute-start | bytes 1769480 | tf_op jit(solution)/shard_map/ppermute | solution.py:33
  255.9 29.1 %collective-permute-start.69 = (bf16[4,192,768]{2,1,0:T(8,128)(2,1)}, bf16[4,192,768]{2,1,0:T(8,128)(2,1)}, u32[]{:S(2)}, u32[]{:S(2)}) collective-permute-start(bf16[4,192,768]{2,1,0:T(8,128)(2,1)} %fusion.7), channel_id=1, source_target_pairs={{0,8},{4,12},{8,0},{12,4},{1,9},{5,13},{9,1},{13,5},{2,10},{6,14},... | collective-permute-start | bytes 3538952 | tf_op jit(solution)/shard_map/ppermute | solution.py:37
  270.5 39.4 %collective-permute-start.63 = (bf16[4,96,1536]{2,1,0:T(8,128)(2,1)}, bf16[4,96,1536]{2,1,0:T(8,128)(2,1)}, u32[]{:S(2)}, u32[]{:S(2)}) collective-permute-start(bf16[4,96,1536]{2,1,0:T(8,128)(2,1)} %fusion.6), channel_id=1, source_target_pairs={{0,8},{4,12},{8,0},{12,4},{1,9},{5,13},{9,1},{13,5},{2,10},{6,14},... | collective-permute-start | bytes 3538952 | tf_op jit(solution)/shard_map/ppermute | solution.py:37
  273.6 133.7 %collective-permute-start.44 = (bf16[3,256,768]{2,1,0:T(8,128)(2,1)}, bf16[3,256,768]{2,1,0:T(8,128)(2,1)}, u32[]{:S(2)}, u32[]{:S(2)}) collective-permute-start(bf16[3,256,768]{2,1,0:T(8,128)(2,1)} %copy-done.7), channel_id=1, source_target_pairs={{0,4},{4,0},{8,12},{12,8},{1,5},{5,1},{9,13},{13,9},{2,6},{6,2},{1... | collective-permute-start | bytes 3538952 | tf_op jit(solution)/shard_map/ppermute | solution.py:33
  275.2 36.6 %collective-permute-start.42 = (bf16[3,256,768]{2,1,0:T(8,128)(2,1)S(1)}, bf16[3,256,768]{2,1,0:T(8,128)(2,1)S(1)}, u32[]{:S(2)}, u32[]{:S(2)}) collective-permute-start(bf16[3,256,768]{2,1,0:T(8,128)(2,1)S(1)} %copy-done.23), channel_id=1, source_target_pairs={{0,4},{4,0},{8,12},{12,8},{1,5},{5,1},{9,13},{13,9},{2,6},{6,2},{1... | collective-permute-start | bytes 3538952 | tf_op jit(solution)/shard_map/ppermute | solution.py:33
  288.2 48.0 %collective-permute-start.70 = (bf16[192,768]{1,0:T(8,128)(2,1)}, bf16[192,768]{1,0:T(8,128)(2,1)}, u32[]{:S(2)}, u32[]{:S(2)}) collective-permute-start(bf16[192,768]{1,0:T(8,128)(2,1)} %fusion.25), channel_id=1, source_target_pairs={{0,1},{1,2},{2,3},{3,0},{4,5},{5,6},{6,7},{7,4},{8,9},{9,10},{10,1... | collective-permute-start | bytes 884744 | tf_op jit(solution)/shard_map/ppermute | solution.py:42
  311.6 38.3 %collective-permute-start.64 = (bf16[96,1536]{1,0:T(8,128)(2,1)S(1)}, bf16[96,1536]{1,0:T(8,128)(2,1)}, u32[]{:S(2)}, u32[]{:S(2)}) collective-permute-start(bf16[96,1536]{1,0:T(8,128)(2,1)S(1)} %fusion.24), channel_id=1, source_target_pairs={{0,1},{1,2},{2,3},{3,0},{4,5},{5,6},{6,7},{7,4},{8,9},{9,10},{10,1... | collective-permute-start | bytes 884744 | tf_op jit(solution)/shard_map/ppermute | solution.py:42
  328.5 7.5 %collective-permute-start.58 = (bf16[192,384]{1,0:T(8,128)(2,1)S(1)}, bf16[192,384]{1,0:T(8,128)(2,1)S(1)}, u32[]{:S(2)}, u32[]{:S(2)}) collective-permute-start(bf16[192,384]{1,0:T(8,128)(2,1)S(1)} %fusion.32), channel_id=1, source_target_pairs={{0,1},{1,2},{2,3},{3,0},{4,5},{5,6},{6,7},{7,4},{8,9},{9,10},{10,1... | collective-permute-start | bytes 442376 | tf_op jit(solution)/shard_map/ppermute | solution.py:42
  333.5 28.4 %collective-permute-start.53 = (bf16[192,1152]{1,0:T(8,128)(2,1)S(1)}, bf16[192,1152]{1,0:T(8,128)(2,1)S(1)}, u32[]{:S(2)}, u32[]{:S(2)}) collective-permute-start(bf16[192,1152]{1,0:T(8,128)(2,1)S(1)} %fusion.23), channel_id=1, source_target_pairs={{0,1},{1,2},{2,3},{3,0},{4,5},{5,6},{6,7},{7,4},{8,9},{9,10},{10,1... | collective-permute-start | bytes 1327112 | tf_op jit(solution)/shard_map/ppermute | solution.py:42
  336.1 66.8 %collective-permute-start.43 = (bf16[3,256,768]{2,1,0:T(8,128)(2,1)}, bf16[3,256,768]{2,1,0:T(8,128)(2,1)}, u32[]{:S(2)}, u32[]{:S(2)}) collective-permute-start(bf16[3,256,768]{2,1,0:T(8,128)(2,1)} %get-tuple-element.53.own_ref), channel_id=1, source_target_pairs={{0,4},{4,0},{8,12},{12,8},{1,5},{5,1},{9,13},{13,9},{2,6},{6,2},{1... | collective-permute-start | bytes 3538952 | tf_op jit(solution)/shard_map/ppermute | solution.py:33
  336.1 13.7 %collective-permute-start.59 = (bf16[192,384]{1,0:T(8,128)(2,1)S(1)}, bf16[192,384]{1,0:T(8,128)(2,1)S(1)}, u32[]{:S(2)}, u32[]{:S(2)}) collective-permute-start(bf16[192,384]{1,0:T(8,128)(2,1)S(1)} %fusion.29), channel_id=1, source_target_pairs={{0,1},{1,2},{2,3},{3,0},{4,5},{5,6},{6,7},{7,4},{8,9},{9,10},{10,1... | collective-permute-start | bytes 442376 | tf_op jit(solution)/shard_map/ppermute | solution.py:42
  349.8 12.9 %collective-permute-start.71 = (bf16[192,768]{1,0:T(8,128)(2,1)S(1)}, bf16[192,768]{1,0:T(8,128)(2,1)S(1)}, u32[]{:S(2)}, u32[]{:S(2)}) collective-permute-start(bf16[192,768]{1,0:T(8,128)(2,1)S(1)} %fusion.16), channel_id=1, source_target_pairs={{0,1},{1,2},{2,3},{3,0},{4,5},{5,6},{6,7},{7,4},{8,9},{9,10},{10,1... | collective-permute-start | bytes 884744 | tf_op jit(solution)/shard_map/ppermute | solution.py:42
  349.8 12.1 %collective-permute-start.60 = (bf16[192,384]{1,0:T(8,128)(2,1)S(1)}, bf16[192,384]{1,0:T(8,128)(2,1)S(1)}, u32[]{:S(2)}, u32[]{:S(2)}) collective-permute-start(bf16[192,384]{1,0:T(8,128)(2,1)S(1)} %fusion.30), channel_id=1, source_target_pairs={{0,1},{1,2},{2,3},{3,0},{4,5},{5,6},{6,7},{7,4},{8,9},{9,10},{10,1... | collective-permute-start | bytes 442376 | tf_op jit(solution)/shard_map/ppermute | solution.py:42
  361.9 11.7 %collective-permute-start.65 = (bf16[96,1536]{1,0:T(8,128)(2,1)S(1)}, bf16[96,1536]{1,0:T(8,128)(2,1)S(1)}, u32[]{:S(2)}, u32[]{:S(2)}) collective-permute-start(bf16[96,1536]{1,0:T(8,128)(2,1)S(1)} %fusion.19), channel_id=1, source_target_pairs={{0,1},{1,2},{2,3},{3,0},{4,5},{5,6},{6,7},{7,4},{8,9},{9,10},{10,1... | collective-permute-start | bytes 884744 | tf_op jit(solution)/shard_map/ppermute | solution.py:42
  362.0 5.2 %collective-permute-start.61 = (bf16[192,384]{1,0:T(8,128)(2,1)S(1)}, bf16[192,384]{1,0:T(8,128)(2,1)S(1)}, u32[]{:S(2)}, u32[]{:S(2)}) collective-permute-start(bf16[192,384]{1,0:T(8,128)(2,1)S(1)} %fusion.31), channel_id=1, source_target_pairs={{0,8},{4,12},{8,0},{12,4},{1,9},{5,13},{9,1},{13,5},{2,10},{6,14},... | collective-permute-start | bytes 442376 | tf_op jit(solution)/shard_map/ppermute | solution.py:37
  362.6 31.3 %collective-permute-start.54 = (bf16[192,1152]{1,0:T(8,128)(2,1)S(1)}, bf16[192,1152]{1,0:T(8,128)(2,1)}, u32[]{:S(2)}, u32[]{:S(2)}) collective-permute-start(bf16[192,1152]{1,0:T(8,128)(2,1)S(1)} %fusion.13), channel_id=1, source_target_pairs={{0,1},{1,2},{2,3},{3,0},{4,5},{5,6},{6,7},{7,4},{8,9},{9,10},{10,1... | collective-permute-start | bytes 1327112 | tf_op jit(solution)/shard_map/ppermute | solution.py:42
  367.2 21.8 %collective-permute-start.72 = (bf16[192,768]{1,0:T(8,128)(2,1)}, bf16[192,768]{1,0:T(8,128)(2,1)}, u32[]{:S(2)}, u32[]{:S(2)}) collective-permute-start(bf16[192,768]{1,0:T(8,128)(2,1)} %fusion.17), channel_id=1, source_target_pairs={{0,1},{1,2},{2,3},{3,0},{4,5},{5,6},{6,7},{7,4},{8,9},{9,10},{10,1... | collective-permute-start | bytes 884744 | tf_op jit(solution)/shard_map/ppermute | solution.py:42
  375.0 17.1 %collective-permute-start.66 = (bf16[96,1536]{1,0:T(8,128)(2,1)}, bf16[96,1536]{1,0:T(8,128)(2,1)}, u32[]{:S(2)}, u32[]{:S(2)}) collective-permute-start(bf16[96,1536]{1,0:T(8,128)(2,1)} %fusion.20), channel_id=1, source_target_pairs={{0,1},{1,2},{2,3},{3,0},{4,5},{5,6},{6,7},{7,4},{8,9},{9,10},{10,1... | collective-permute-start | bytes 884744 | tf_op jit(solution)/shard_map/ppermute | solution.py:42
  390.2 8.5 %collective-permute-start.73 = (bf16[192,768]{1,0:T(8,128)(2,1)S(1)}, bf16[192,768]{1,0:T(8,128)(2,1)S(1)}, u32[]{:S(2)}, u32[]{:S(2)}) collective-permute-start(bf16[192,768]{1,0:T(8,128)(2,1)S(1)} %fusion.18), channel_id=1, source_target_pairs={{0,8},{4,12},{8,0},{12,4},{1,9},{5,13},{9,1},{13,5},{2,10},{6,14},... | collective-permute-start | bytes 884744 | tf_op jit(solution)/shard_map/ppermute | solution.py:37
  393.4 8.5 %collective-permute-start.67 = (bf16[96,1536]{1,0:T(8,128)(2,1)S(1)}, bf16[96,1536]{1,0:T(8,128)(2,1)S(1)}, u32[]{:S(2)}, u32[]{:S(2)}) collective-permute-start(bf16[96,1536]{1,0:T(8,128)(2,1)S(1)} %fusion.21), channel_id=1, source_target_pairs={{0,8},{4,12},{8,0},{12,4},{1,9},{5,13},{9,1},{13,5},{2,10},{6,14},... | collective-permute-start | bytes 884744 | tf_op jit(solution)/shard_map/ppermute | solution.py:37
  396.1 49.3 %collective-permute-start.55 = (bf16[192,1152]{1,0:T(8,128)(2,1)}, bf16[192,1152]{1,0:T(8,128)(2,1)S(1)}, u32[]{:S(2)}, u32[]{:S(2)}) collective-permute-start(bf16[192,1152]{1,0:T(8,128)(2,1)} %fusion.14), channel_id=1, source_target_pairs={{0,1},{1,2},{2,3},{3,0},{4,5},{5,6},{6,7},{7,4},{8,9},{9,10},{10,1... | collective-permute-start | bytes 1327112 | tf_op jit(solution)/shard_map/ppermute | solution.py:42
  399.8 61.0 %collective-permute-start.74 = (bf16[384,768]{1,0:T(8,128)(2,1)}, bf16[384,768]{1,0:T(8,128)(2,1)}, u32[]{:S(2)}, u32[]{:S(2)}) collective-permute-start(bf16[384,768]{1,0:T(8,128)(2,1)} %maximum_select_fusion.4), channel_id=1, source_target_pairs={{0,4},{4,0},{8,12},{12,8},{1,5},{5,1},{9,13},{13,9},{2,6},{6,2},{1... | collective-permute-start | bytes 1769480 | tf_op jit(solution)/shard_map/ppermute | solution.py:33
  402.8 47.3 %collective-permute-start.68 = (bf16[192,1536]{1,0:T(8,128)(2,1)}, bf16[192,1536]{1,0:T(8,128)(2,1)}, u32[]{:S(2)}, u32[]{:S(2)}) collective-permute-start(bf16[192,1536]{1,0:T(8,128)(2,1)} %maximum_select_fusion.3), channel_id=1, source_target_pairs={{0,4},{4,0},{8,12},{12,8},{1,5},{5,1},{9,13},{13,9},{2,6},{6,2},{1... | collective-permute-start | bytes 1769480 | tf_op jit(solution)/shard_map/ppermute | solution.py:33
  410.9 37.1 %collective-permute-start.45 = (bf16[3,64,768]{2,1,0:T(8,128)(2,1)}, bf16[3,64,768]{2,1,0:T(8,128)(2,1)}, u32[]{:S(2)}, u32[]{:S(2)}) collective-permute-start(bf16[3,64,768]{2,1,0:T(8,128)(2,1)} %fusion.26), channel_id=1, source_target_pairs={{0,8},{4,12},{8,0},{12,4},{1,9},{5,13},{9,1},{13,5},{2,10},{6,14},... | collective-permute-start | bytes 884744 | tf_op jit(solution)/shard_map/ppermute | solution.py:37
  417.9 5.6 %collective-permute-start.48 = (bf16[6,4608]{1,0:T(8,128)(2,1)S(1)}, bf16[6,4608]{1,0:T(8,128)(2,1)S(1)}, u32[]{:S(2)}, u32[]{:S(2)}) collective-permute-start(bf16[6,4608]{1,0:T(8,128)(2,1)S(1)} %maximum_select_fusion.6), channel_id=1, source_target_pairs={{0,2},{1,3},{2,0},{3,1},{4,6},{5,7},{6,4},{7,5},{8,10},{9,11},{10,... | collective-permute-start | bytes 165896 | tf_op jit(solution)/shard_map/ppermute | solution.py:42
  423.5 6.2 %collective-permute-start.49 = (bf16[6,4608]{1,0:T(8,128)(2,1)S(1)}, bf16[6,4608]{1,0:T(8,128)(2,1)S(1)}, u32[]{:S(2)}, u32[]{:S(2)}) collective-permute-start(bf16[6,4608]{1,0:T(8,128)(2,1)S(1)} %maximum_select_fusion.6), channel_id=1, source_target_pairs={{0,1},{1,2},{2,3},{3,0},{4,5},{5,6},{6,7},{7,4},{8,9},{9,10},{10,1... | collective-permute-start | bytes 165896 | tf_op jit(solution)/shard_map/ppermute | solution.py:42
  438.8 5.7 %collective-permute-start.52 = (f32[6,192]{1,0:T(8,128)S(1)}, f32[6,192]{1,0:T(8,128)S(1)}, u32[]{:S(2)}, u32[]{:S(2)}) collective-permute-start(f32[6,192]{1,0:T(8,128)S(1)} %get-tuple-element.131), channel_id=1, source_target_pairs={{0,1},{1,2},{2,3},{3,0},{4,5},{5,6},{6,7},{7,4},{8,9},{9,10},{10,1... | collective-permute-start | bytes 13832 | tf_op jit(solution)/shard_map/ppermute | solution.py:42
  447.5 12.0 %collective-permute-start.56 = (bf16[192,1152]{1,0:T(8,128)(2,1)}, bf16[192,1152]{1,0:T(8,128)(2,1)}, u32[]{:S(2)}, u32[]{:S(2)}) collective-permute-start(bf16[192,1152]{1,0:T(8,128)(2,1)} %fusion.15), channel_id=1, source_target_pairs={{0,8},{4,12},{8,0},{12,4},{1,9},{5,13},{9,1},{13,5},{2,10},{6,14},... | collective-permute-start | bytes 1327112 | tf_op jit(solution)/shard_map/ppermute | solution.py:37
  (66 other events, 644.7 us)
